TPU v7x, 32 devices: a whole 2x2x4 slice. The times are simulated.
32 devices in a mesh: row: 4 (over y, core), col: 8 (over z, x).
Axes of the slice: x: 2, y: 2, z: 4, core: 2. Of those that a mesh axis runs over, the one named last changes fastest.
Arguments:
- grad_out: bfloat16 [1024, 16384], P('col', 'row'), may hold values from -0.1875 to 0.1875
- activations: bfloat16 [1024, 16384], P('row', 'col'), may hold values from -6 to 6
- projector: bfloat16 [16384, 1024], P('row'), may hold values from -0.046875 to 0.046875
- weight: float32 [16384, 16384], P('row', 'col'), may hold values from -6 to 6
- first_moment: float32 [1024, 16384], P('row', 'col'), may hold values from -3 to 3
- second_moment: float32 [1024, 16384], P('row', 'col'), may hold values from 0.25 to 4
Outputs:
- new_weight: float32 [16384, 16384], P('row', 'col')
- new_first: float32 [1024, 16384], P('row', 'col')
- new_second: float32 [1024, 16384], P('row', 'col')
All inputs are finite; a program needn't handle non-finite values.
Results may differ from a plain program's by a relative error of at most 0.0015.
Values may be sent and summed in bfloat16 or wider, within the bound.
No kernel may reach another device: no remote copies, remote signals or barrier semaphores. Data moves between devices by JAX's collectives and lax.ppermute only.
A program may use at most 192 MiB of HBM per device.

v0:
```python
import jax
import jax.numpy as jnp
from jax import lax
from jax.sharding import PartitionSpec as P

STEP = 10


first_decay = 0.9
second_decay = 0.99
adam_epsilon = 1e-08
learn_rate = 4.0


def split_parts(values):
    upper = values.astype(jnp.bfloat16)
    lower = (values - upper.astype(jnp.float32)).astype(jnp.bfloat16)
    return (upper, lower)


def product_pair(left, right_parts, dims):
    first = lax.dot_general(left, right_parts[0], dims, preferred_element_type=jnp.float32)
    second = lax.dot_general(left, right_parts[1], dims, preferred_element_type=jnp.float32)
    return first + second


def body(grad_out, activations, projector, weight, first_moment, second_moment):
    token_inputs = lax.all_gather(activations, "row", axis=0, tiled=True)
    lowered = jnp.dot(grad_out, projector, preferred_element_type=jnp.float32)
    shares = lax.psum_scatter(lowered, "row", scatter_dimension=1, tiled=True)
    upper, lower = split_parts(lax.all_gather(shares, "col", axis=0, tiled=True))
    dims = (((0,), (0,)), ((), ()))
    first = lax.dot_general(upper, token_inputs, dims, preferred_element_type=jnp.float32)
    second = lax.dot_general(lower, token_inputs, dims, preferred_element_type=jnp.float32)
    lowgrad = first + second
    new_first = first_decay * first_moment + (1.0 - first_decay) * lowgrad
    new_second = second_decay * second_moment + (1.0 - second_decay) * lowgrad * lowgrad
    corrected_first = new_first / (1.0 - first_decay**STEP)
    corrected_second = new_second / (1.0 - second_decay**STEP)
    direction = corrected_first / (jnp.sqrt(corrected_second) + adam_epsilon)
    new_weight = weight - learn_rate * product_pair(
        projector,
        split_parts(lax.all_gather(direction, "row", axis=0, tiled=True)),
        (((1,), (0,)), ((), ())),
    )
    return (new_weight, new_first, new_second)


def solution(mesh):
    in_specs = (
        P("col", "row"),
        P("row", "col"),
        P("row", None),
        P("row", "col"),
        P("row", "col"),
        P("row", "col"),
    )
    out_specs = (P("row", "col"), P("row", "col"), P("row", "col"))
    return jax.shard_map(body, mesh=mesh, in_specs=in_specs, out_specs=out_specs, check_vma=False)
```

profile of v0, /device:TPU:0, one launch (start us, length us, event | category | flops | bytes accessed | tf_op | source)
XLA Modules:
  0.0 304.3 jit_solution(1795932703378772696)
XLA Ops:
  7.2 0.0 copy-start
  7.2 0.0 reduce-scatter.2.cloned.1.call-start
  7.2 1.2 copy-done
  8.4 5.4 %fusion.8 = f32[128,1024]{1,0:T(8,128)} fusion(bf16[128,4096]{1,0:T(8,128)(2,1)S(1)} %copy-done, bf16[4096,1024]{1,0:T(8,128)(2,1)} %param.8), kind=kOutput, calls=%fused_computation.14 | convolution fusion | flops 1073741824 | bytes 9961472 | tf_op jit(solution)/shard_map/dot_general | solution.py:29
  13.8 0.0 reduce-scatter.2.cloned.1.call-update
  13.9 0.0 all-gather.4.cloned.1.call-start
  13.9 24.5 %reduce-scatter.2.cloned.1.call-done = f32[128,256]{1,0:T(8,128)} async-done(((f32[128,1024]{1,0:T(8,128)}), f32[128,256]{1,0:T(8,128)}) %reduce-scatter.2.cloned.1.call-update) | async-done | bytes 131088 | tf_op jit(solution)/shard_map/reduce_scatter | solution.py:30
  38.4 0.0 all-gather.4.cloned.1.call-update
  38.4 0.0 copy-start.4
  38.4 0.0 all-gather.6.cloned.1.call-start
  38.4 0.7 all-gather.6.cloned.1.call-update
  39.1 0.0 all-gather.8.cloned.1.call-start
  39.2 41.7 %all-gather.4.cloned.1.call-done = f32[1024,256]{1,0:T(8,128)} async-done(((f32[128,256]{1,0:T(8,128)}), f32[1024,256]{1,0:T(8,128)}) %all-gather.4.cloned.1.call-update) | async-done | bytes 1048592 | tf_op jit(solution)/shard_map/all_gather | solution.py:31
  80.9 34.9 %all-gather.6.cloned.1.call-done = bf16[1024,2048]{1,0:T(8,128)(2,1)} async-done(((bf16[256,2048]{1,0:T(8,128)(2,1)}), bf16[1024,2048]{1,0:T(8,128)(2,1)}) %all-gather.6.cloned.1.call-update) | async-done | bytes 4194320 | tf_op jit(solution)/shard_map/all_gather | solution.py:28
  115.8 3.9 %fusion.5 = f32[256,2048]{1,0:T(8,128)S(1)} fusion(bf16[1024,2048]{1,0:T(8,128)(2,1)} %all-gather.6.cloned.1.call-done, f32[1024,256]{1,0:T(8,128)} %all-gather.4.cloned.1.call-done), kind=kOutput, calls=%fused_computation.12 | convolution fusion | flops 1074003968 | bytes 7340032 | tf_op jit(solution)/shard_map/dot_general | solution.py:33
  119.7 0.0 copy-done.4
  119.8 6.9 %add_divide_fusion = (f32[256,2048]{1,0:T(8,128)}, f32[256,2048]{1,0:T(8,128)}, f32[256,2048]{1,0:T(8,128)}) fusion(f32[256,2048]{1,0:T(8,128)S(1)} %copy-done.4, f32[256,2048]{1,0:T(8,128)} %param.11, f32[256,2048]{1,0:T(8,128)S(1)} %fusion.5, bf16[1024,2048]{1,0:T(8,128)(2,1)S(1)} %copy-done.2, f32[1024,256]{1,0:T(8,128)S(1)} %copy-done.3), kind=kOutput, calls=%fused_computation.8 | convolution fusion | flops 1081081856 | bytes 17825792 | tf_op jit(solution)/shard_map/dot_general | solution.py:34
  126.6 0.0 all-gather.8.cloned.1.call-update
  126.7 31.6 %copy.9 = f32[4096,2048]{0,1:T(8,128)} copy(f32[4096,2048]{1,0:T(8,128)} %param.9) | data formatting | bytes 67108864 | tf_op args[3]
  158.3 26.8 %all-gather.8.cloned.1.call-done = f32[1024,2048]{1,0:T(8,128)} async-done(((f32[256,2048]{1,0:T(8,128)}), f32[1024,2048]{1,0:T(8,128)}) %all-gather.8.cloned.1.call-update) | async-done | bytes 8388624 | tf_op jit(solution)/shard_map/all_gather | solution.py:43
  185.1 25.7 %fusion.2 = f32[2048,4096]{1,0:T(8,128)} fusion(bf16[4096,1024]{1,0:T(8,128)(2,1)} %param.8, f32[1024,2048]{1,0:T(8,128)} %all-gather.8.cloned.1.call-done), kind=kOutput, calls=%fused_computation.6 | convolution fusion | flops 17181966336 | bytes 50331648 | tf_op jit(solution)/shard_map/dot_general | solution.py:22
  210.8 53.5 %bitcast_subtract_fusion = f32[4096,2048]{0,1:T(8,128)} fusion(f32[4096,2048]{0,1:T(8,128)} %copy.9, f32[2048,4096]{1,0:T(8,128)} %fusion.2, bf16[4096,1024]{1,0:T(8,128)(2,1)} %param.8, f32[1024,2048]{1,0:T(8,128)} %all-gather.8.cloned.1.call-done), kind=kOutput, calls=%fused_computation | convolution fusion | flops 17213423616 | bytes 117440512 | tf_op jit(solution)/shard_map/dot_general | solution.py:23
  264.3 33.4 %copy.10 = f32[4096,2048]{1,0:T(8,128)} copy(f32[4096,2048]{0,1:T(8,128)} %bitcast_subtract_fusion) | data formatting | bytes 67108864
  297.7 0.0 copy-done.1
  (5 shorter events, 0.0 us)
Async XLA Ops:
  7.2 1.2 copy-start
  7.2 31.2 %reduce-scatter.2.cloned.1.call-start = ((), (), s32[]{:S(2)}) async-start(), calls=%async_computation.1 | async-start | bytes 655360 | tf_op jit(solution)/shard_map/reduce_scatter | solution.py:30
  13.9 67.0 %all-gather.4.cloned.1.call-start = ((), (), s32[]{:S(2)}) async-start(), calls=%async_computation.2 | async-start | bytes 1179648 | tf_op jit(solution)/shard_map/all_gather | solution.py:31
  38.4 81.4 %copy-start.4 = (f32[256,2048]{1,0:T(8,128)S(1)}, f32[256,2048]{1,0:T(8,128)}, u32[]{:S(2)}) copy-start(f32[256,2048]{1,0:T(8,128)} %param.10) | copy-start | bytes 6291460
  38.4 77.4 %all-gather.6.cloned.1.call-start = ((), (), s32[]{:S(2)}) async-start(), calls=%async_computation.3 | async-start | bytes 5242880 | tf_op jit(solution)/shard_map/all_gather | solution.py:28
  39.1 146.0 %all-gather.8.cloned.1.call-start = ((), (), s32[]{:S(2)}) async-start(), calls=%async_computation.4 | async-start | bytes 10485760 | tf_op jit(solution)/shard_map/all_gather | solution.py:43
  80.9 38.9 %copy-start.3 = (f32[1024,256]{1,0:T(8,128)S(1)}, f32[1024,256]{1,0:T(8,128)}, u32[]{:S(2)}) copy-start(f32[1024,256]{1,0:T(8,128)} %all-gather.4.cloned.1.call-done) | copy-start | bytes 3145732
  115.8 3.9 %copy-start.2 = (bf16[1024,2048]{1,0:T(8,128)(2,1)S(1)}, bf16[1024,2048]{1,0:T(8,128)(2,1)}, u32[]{:S(2)}) copy-start(bf16[1024,2048]{1,0:T(8,128)(2,1)} %all-gather.6.cloned.1.call-done) | copy-start | bytes 12582916
  264.3 33.4 %copy-start.1 = (bf16[128,4096]{1,0:T(8,128)(2,1)S(1)}, bf16[128,4096]{1,0:T(8,128)(2,1)}, u32[]{:S(2)}) copy-start(bf16[128,4096]{1,0:T(8,128)(2,1)} %param.6) | copy-start | bytes 3145732
Sparse Core Ops, SparseCore 0:
  14.0 24.3 reduce-scatter.1
  40.7 40.1 all-gather.3
  82.5 33.2 all-gather.5
  126.8 58.2 all-gather.7
where the time goes:
time: 305 us; the launch traced here: 304 us
  waiting for transfers between devices  129 us (42%)
  matrix products  95.4 us (31%)
  local copies, waits for them, and re-layouts  66.3 us (22%)
  between operations  13.8 us (5%)
    unnamed x12, local copies, waits for them, and re-layouts  66.3 us
    dot_general x1, matrix products, product_pair(): lax.dot_general(left, right_parts[1], dims, preferred_element_type=jnp.fl...  53.5 us
    all_gather x1, waiting for transfers between devices, body(): lax.all_gather(shares, 'col', axis=0, tiled=True)  41.7 us
    all_gather x1, waiting for transfers between devices, body(): token_inputs = lax.all_gather(activations, 'row', axis=0, tiled=True)  34.9 us
    all_gather x1, waiting for transfers between devices, body(): lax.all_gather(direction, 'row', axis=0, tiled=True)  26.8 us
    dot_general x1, matrix products, product_pair(): lax.dot_general(left, right_parts[0], dims, preferred_element_type=jnp.fl...  25.7 us
    reduce_scatter x1, waiting for transfers between devices, body(): shares = lax.psum_scatter(lowered, 'row', scatter_dimension=1, tiled=True)  24.5 us
    dot_general x1, matrix products, body(): lax.dot_general(lower, token_inputs, dims, preferred_element_type=jnp.flo...  6.87 us
  transfers between devices with their start and end apart: 4, of which 4 were waited for; matrix products, arithmetic and copies ran while one was open for 10% of the time, Pallas kernels for 0%

commit v1 on v0

v1 whole, which is shorter than its diff:
```python
import functools

import jax
import jax.numpy as jnp
from jax import lax
from jax.experimental import pallas as pl
from jax.experimental.pallas import tpu as pltpu
from jax.sharding import PartitionSpec as P

STEP = 10

first_decay = 0.9
second_decay = 0.99
adam_epsilon = 1e-08
learn_rate = 4.0

MIB = 1 << 20
VMEM = pl.BlockSpec(memory_space=pltpu.VMEM)
ANY = pl.BlockSpec(memory_space=pltpu.HBM)
MARK = jax.ShapeDtypeStruct((16, 128), jnp.bfloat16)


def exchange(values, axis, size, mask):
    return lax.ppermute(values, axis, [(i, i ^ mask) for i in range(size)])


def parameters(mib):
    return pltpu.CompilerParams(vmem_limit_bytes=mib * MIB)


def cost(flops, moved):
    return pl.CostEstimate(flops=flops, bytes_accessed=moved, transcendentals=0)


def lowered_kernel(height, cuts, grad_hbm, basis_hbm, input_hbm, *refs):
    n_cuts = len(cuts)
    out_refs, input_refs = refs[: -n_cuts - 4], refs[-n_cuts - 4 : -4]
    grad_ref, basis_ref, total_ref, sems = refs[-4:]
    me = lax.axis_index("row")
    count = basis_ref.shape[0] // height

    def rows(step):
        return slice(step * height, (step + 1) * height)

    copies = [pltpu.make_async_copy(grad_hbm, grad_ref, sems.at[0])]
    for step in range(count):
        copies.append(pltpu.make_async_copy(basis_hbm.at[rows(step)], basis_ref.at[rows(step)], sems.at[1 + step]))
    for index, (at, width) in enumerate(cuts):
        here = slice(at, at + width)
        copies.append(pltpu.make_async_copy(input_hbm.at[:, here], input_refs[index], sems.at[1 + count + index]))
    for copy in copies:
        copy.start()
    copies[0].wait()
    for step in range(count):
        copies[1 + step].wait()
        term = jnp.dot(grad_ref[:, rows(step)], basis_ref[rows(step), :], preferred_element_type=jnp.float32)
        if step == 0:
            total_ref[...] = term
        else:
            total_ref[...] += term
    width = out_refs[0].shape[1]
    for mask, out_ref in enumerate(out_refs):
        columns = pl.ds(pl.multiple_of((me ^ mask) * width, width), width)
        out_ref[...] = total_ref[:, columns].astype(out_ref.dtype)
    for copy in copies[1 + count :]:
        copy.wait()


def lowered_terms(grad_out, projector, activations, cuts, n_row):
    tokens, ranks = grad_out.shape[0], projector.shape[1] // n_row
    height = min(512, projector.shape[0])
    count = projector.shape[0] // height
    kinds = [jnp.float32] + [jnp.bfloat16] * (n_row - 1)
    results = pl.pallas_call(
        functools.partial(lowered_kernel, height, cuts),
        out_shape=[jax.ShapeDtypeStruct((tokens, ranks), kind) for kind in kinds]
        + [pltpu.VMEM((activations.shape[0], width), activations.dtype) for _, width in cuts],
        in_specs=[ANY] * 3,
        out_specs=[VMEM] * (n_row + len(cuts)),
        scratch_shapes=[
            pltpu.VMEM(grad_out.shape, grad_out.dtype),
            pltpu.VMEM(projector.shape, projector.dtype),
            pltpu.VMEM((tokens, projector.shape[1]), jnp.float32),
            pltpu.SemaphoreType.DMA((1 + count + len(cuts),)),
        ],
        compiler_params=parameters(14),
        cost_estimate=cost(1, 1),
        name="lowered_terms",
    )(grad_out, projector, activations)
    return results[:n_row], results[n_row:]


def load_kernel(offset, height, weight_hbm, mark_in, chunk_ref, mark_ref, sems):
    del mark_in
    width = chunk_ref.shape[1]
    copies = []
    for step in range(chunk_ref.shape[0] // height):
        rows = slice(step * height, (step + 1) * height)
        source = weight_hbm.at[rows, offset : offset + width]
        copies.append(pltpu.make_async_copy(source, chunk_ref.at[rows], sems.at[step]))
    for copy in copies:
        copy.start()
    mark_ref[...] = jnp.zeros_like(mark_ref)
    for copy in copies:
        copy.wait()


def load_weight(weight, offset, width, mark):
    rows = weight.shape[0]
    height = min(1024, rows)
    return pl.pallas_call(
        functools.partial(load_kernel, offset, height),
        out_shape=[pltpu.VMEM((rows, width), weight.dtype), MARK],
        in_specs=[ANY, VMEM],
        out_specs=[VMEM, VMEM],
        scratch_shapes=[pltpu.SemaphoreType.DMA((rows // height,))],
        compiler_params=parameters(2),
        cost_estimate=cost(1, 4 * rows * width),
        name="load_weight",
    )(weight, mark)


def share_kernel(n_terms, *refs):
    total = refs[0][...]
    for ref in refs[1:n_terms]:
        total = total + ref[...].astype(jnp.float32)
    refs[-1][...] = total.T.astype(jnp.bfloat16)


def share_sum(terms, marks):
    tokens, ranks = terms[0].shape
    return pl.pallas_call(
        functools.partial(share_kernel, len(terms)),
        out_shape=jax.ShapeDtypeStruct((ranks, tokens), jnp.bfloat16),
        in_specs=[VMEM] * (len(terms) + len(marks)),
        out_specs=VMEM,
        compiler_params=parameters(4),
        cost_estimate=cost(1, 1),
        name="share_sum",
    )(*terms, *marks)


def stack_kernel(n_parts, *refs):
    out_ref, mark_ref = refs[-2:]
    height = refs[0].shape[0]
    for index, part in enumerate(refs[:n_parts]):
        out_ref[index * height : (index + 1) * height] = part[...]
    mark_ref[...] = jnp.zeros_like(mark_ref)


def stack(parts, marks):
    height, width = parts[0].shape
    return pl.pallas_call(
        functools.partial(stack_kernel, len(parts)),
        out_shape=[jax.ShapeDtypeStruct((height * len(parts), width), parts[0].dtype), MARK],
        in_specs=[VMEM] * (len(parts) + len(marks)),
        out_specs=[VMEM, VMEM],
        compiler_params=parameters(4),
        cost_estimate=cost(1, 1),
        name="stack",
    )(*parts, *marks)


def adam_kernel(n_row, n_pieces, n_skip, offset, step, cuts, *refs):
    pieces, refs = refs[:n_pieces], refs[n_pieces:]
    inputs, refs = refs[:n_row], refs[n_row:]
    first_hbm, second_hbm, refs = refs[0], refs[1], refs[2 + n_skip :]
    new_first_ref, new_second_ref, direction_ref, mark_ref = refs[:4]
    part_refs, (lowered_ref, firsts, seconds, sems) = refs[4:-4], refs[-4:]
    mark_ref[...] = jnp.zeros_like(mark_ref)
    depth, width = inputs[0].shape

    def moment_copies(number):
        there = slice(offset + number * step, offset + (number + 1) * step)
        return [
            pltpu.make_async_copy(source.at[:, there], target.at[number], sems.at[number, which])
            for which, (source, target) in enumerate(((first_hbm, firsts), (second_hbm, seconds)))
        ]

    for number in range(width // step):
        for copy in moment_copies(number):
            copy.start()
    row, col = lax.axis_index("row"), lax.axis_index("col")
    ranks, span = lowered_ref.shape[0], pieces[0].shape[1]
    if n_pieces > 1:
        for mask in range(lowered_ref.shape[1] // span):
            columns = pl.ds(pl.multiple_of((col ^ mask) * span, span), span)
            held = pieces[mask % 2]
            lowered_ref[:, columns] = held[mask // 2 * ranks : (mask // 2 + 1) * ranks, :]
    else:
        lowered_ref[...] = pieces[0][...]
    copies = []
    for number, at in enumerate(range(0, width, step)):
        here = slice(at, at + step)
        there = slice(offset + at, offset + at + step)
        lowgrad = None
        for mask, block in enumerate(inputs):
            columns = pl.ds(pl.multiple_of((row ^ mask) * depth, depth), depth)
            term = jnp.dot(lowered_ref[:, columns], block[:, here], preferred_element_type=jnp.float32)
            lowgrad = term if lowgrad is None else lowgrad + term
        for copy in moment_copies(number):
            copy.wait()
        new_first = first_decay * firsts[number] + (1.0 - first_decay) * lowgrad
        new_second = second_decay * seconds[number] + (1.0 - second_decay) * lowgrad * lowgrad
        firsts[number] = new_first
        seconds[number] = new_second
        for which, (source, target) in enumerate(((firsts, new_first_ref), (seconds, new_second_ref))):
            copy = pltpu.make_async_copy(source.at[number], target.at[:, there], sems.at[number, 2 + which])
            copy.start()
            copies.append(copy)
        corrected_first = new_first / (1.0 - first_decay**STEP)
        corrected_second = new_second / (1.0 - second_decay**STEP)
        direction = corrected_first / (jnp.sqrt(corrected_second) + adam_epsilon)
        direction_ref[:, here] = (learn_rate * direction).astype(direction_ref.dtype)
    for (at, width), part_ref in zip(cuts, part_refs):
        part_ref[...] = direction_ref[:, at : at + width]
    for copy in copies:
        copy.wait()


def adam_chunk(pieces, inputs, first, second, marks, carried, offset, cuts, n_row):
    ranks = first.shape[0]
    depth, width = inputs[0].shape
    tokens = depth * n_row
    step = min(256, width)
    count = width // step
    n_plain = len(pieces) + n_row + 2 + len(marks)
    return pl.pallas_call(
        functools.partial(adam_kernel, n_row, len(pieces), len(marks) + len(carried), offset, step, cuts),
        out_shape=[
            jax.ShapeDtypeStruct(first.shape, jnp.float32),
            jax.ShapeDtypeStruct(first.shape, jnp.float32),
            jax.ShapeDtypeStruct((ranks, width), jnp.bfloat16),
            MARK,
            *(jax.ShapeDtypeStruct((ranks, part), jnp.bfloat16) for _, part in cuts),
        ],
        in_specs=[VMEM] * (len(pieces) + n_row) + [ANY] * 2 + [VMEM] * len(marks) + [ANY] * len(carried),
        out_specs=[ANY, ANY, VMEM, VMEM] + [VMEM] * len(cuts),
        scratch_shapes=[
            pltpu.VMEM((ranks, tokens), jnp.bfloat16),
            pltpu.VMEM((count, ranks, step), jnp.float32),
            pltpu.VMEM((count, ranks, step), jnp.float32),
            pltpu.SemaphoreType.DMA((count, 4)),
        ],
        input_output_aliases={n_plain: 0, n_plain + 1: 1} if carried else {},
        compiler_params=parameters(6),
        cost_estimate=cost(1, 1),
        name="adam_chunk",
    )(*pieces, *inputs, first, second, *marks, *carried)


def update_kernel(offset, start, height, slots, n_parts, basis_ref, *refs):
    parts, weight_ref = refs[:n_parts], refs[n_parts]
    out_ref, mark_ref, scaled, held, sems = refs[-5:]
    row = lax.axis_index("row")
    ranks, width = parts[0].shape
    there = slice(offset, offset + width)
    count = weight_ref.shape[0] // height
    for mask, part in enumerate(parts):
        here = slice(start, start + width) if mask == 1 else slice(0, width)
        scaled[pl.ds(pl.multiple_of((row ^ mask) * ranks, ranks), ranks), :] = part[:, here]

    def copy(step):
        slot = step % slots
        rows = slice(step * height, (step + 1) * height)
        return pltpu.make_async_copy(held.at[slot], out_ref.at[rows, there], sems.at[slot])

    for step in range(count):
        if step >= slots:
            copy(step - slots).wait()
        rows = slice(step * height, (step + 1) * height)
        update = jnp.dot(basis_ref[rows, :], scaled[...], preferred_element_type=jnp.float32)
        held[step % slots] = weight_ref[rows, :] - update
        copy(step).start()
    mark_ref[...] = jnp.zeros_like(mark_ref)
    for step in range(max(0, count - slots), count):
        copy(step).wait()


def weight_update(projector, parts, weight, shape, carried, offset, start):
    rows = weight.shape[0]
    ranks, width = parts[0].shape
    height = min(512, rows)
    slots = min(3, rows // height)
    n_parts = len(parts)
    return pl.pallas_call(
        functools.partial(update_kernel, offset, start, height, slots, n_parts),
        out_shape=[jax.ShapeDtypeStruct(shape, jnp.float32), MARK],
        in_specs=[VMEM] * (n_parts + 2) + [ANY] * len(carried),
        out_specs=[ANY, VMEM],
        scratch_shapes=[
            pltpu.VMEM((n_parts * ranks, width), jnp.bfloat16),
            pltpu.VMEM((slots, height, width), jnp.float32),
            pltpu.SemaphoreType.DMA((slots,)),
        ],
        input_output_aliases={n_parts + 2: 0} if carried else {},
        compiler_params=parameters(8),
        cost_estimate=cost(2 * rows * ranks * n_parts * width, 4 * rows * width),
        name="weight_update",
    )(projector, *parts, weight, *carried)


def after_kernel(*refs):
    del refs


def after(parts, *marks):
    return pl.pallas_call(
        after_kernel,
        out_shape=[jax.ShapeDtypeStruct(part.shape, part.dtype) for part in parts],
        in_specs=[VMEM] * (len(parts) + len(marks)),
        out_specs=[VMEM] * len(parts),
        input_output_aliases={i: i for i in range(len(parts))},
        compiler_params=parameters(2),
        cost_estimate=cost(1, 1),
        name="after",
    )(*parts, *marks)


def over_y(values, n_row):
    return [exchange(values, "row", n_row, mask) for mask in range(2, n_row, 2)]


def with_core(far, n_row):
    pieces = []
    for piece in far:
        pieces += [piece, exchange(piece, "row", n_row, 1)]
    return pieces


def cut(total, parts):
    chunks, at = [], 0
    for part in parts:
        width = total * part // 16
        if width % 128:
            return [(0, total)]
        chunks.append((at, width))
        at += width
    return chunks


def body(n_row, n_col, grad_out, activations, projector, weight, first_moment, second_moment):
    grad_out, activations, weight, first_moment, second_moment = [
        pltpu.with_memory_space_constraint(values, pltpu.HBM)
        for values in (grad_out, activations, weight, first_moment, second_moment)
    ]
    halves = cut(activations.shape[1], (8, 8))
    parts_of = [cut(width, (8, 8)) for _, width in halves]
    chunks = [(at + start, width) for (at, _), cuts in zip(halves, parts_of) for start, width in cuts]
    loaded = []

    def load(mark):
        if len(loaded) == len(chunks):
            return []
        loaded.append(load_weight(weight, *chunks[len(loaded)], mark))
        return [loaded[-1][1]]

    basis = pltpu.with_memory_space_constraint(projector, pltpu.HBM)
    terms, inputs = lowered_terms(grad_out, basis, activations, halves, n_row)
    marks = load(terms[1])
    received = [exchange(terms[mask], "row", n_row, mask) for mask in range(1, n_row)]
    inputs = after(inputs, *received)
    far_inputs = [over_y(part, n_row) for part in inputs]
    share = share_sum([terms[0]] + received, marks)
    if n_col == 8:
        marks = load(share)
        near = [share] + [exchange(share, "col", n_col, mask) for mask in (2, 4, 6)]
        near, ready = stack(near, marks)
        pieces = [near, exchange(near, "col", n_col, 1)]
    else:
        pieces, ready = [lax.all_gather(share, "col", axis=1, tiled=True)], share
    marks = load(ready)

    moments, directions = [], []
    for (at, _), cuts, part, far in zip(halves, parts_of, inputs, far_inputs):
        part, *far = after([part, *far], ready)
        gathered = [part, exchange(part, "row", n_row, 1)] + with_core(far, n_row)
        new_first, new_second, direction, ready, *parts = adam_chunk(
            pieces, gathered, first_moment, second_moment, marks, moments, at, cuts, n_row
        )
        moments = [new_first, new_second]
        core = exchange(direction, "row", n_row, 1)
        for (start, _), part in zip(cuts, parts):
            directions.append((start, part, core, over_y(part, n_row)))
        marks = load(ready)

    projector = pltpu.with_memory_space_constraint(projector, pltpu.VMEM)
    new_weight, marks = [], [ready, ready]
    for (at, _), (base, _), (start, part, core, far) in zip(chunks, loaded, directions):
        parts = [part, core] + with_core(after(far, marks[-2]), n_row)
        *new_weight, mark = weight_update(projector, parts, base, weight.shape, new_weight, at, start)
        marks.append(mark)
    return (new_weight[0], *moments)


def solution(mesh):
    n_row, n_col = mesh.shape["row"], mesh.shape["col"]
    in_specs = (
        P("col", "row"),
        P("row", "col"),
        P("row", None),
        P("row", "col"),
        P("row", "col"),
        P("row", "col"),
    )
    out_specs = (P("row", "col"), P("row", "col"), P("row", "col"))
    return jax.shard_map(
        functools.partial(body, n_row, n_col),
        mesh=mesh,
        in_specs=in_specs,
        out_specs=out_specs,
        check_vma=False,
    )
```

time: 305 us -> 89.8 us (0.29)
  waiting for transfers between devices: 129 us -> 17.2 us
  matrix products: 95.4 us -> 0 us
  local copies, waits for them, and re-layouts: 66.3 us -> 0.01 us
  Pallas kernels: 0 us -> 54.5 us
  starting transfers between devices: 0.16 us -> 16.9 us
  between operations: 13.8 us -> 0.99 us
    all_gather x3 -> x0, waiting for transfers between devices: 103 us -> none  [the longest x1 41.7 us: body(): lax.all_gather(shares, 'col', axis=0, tiled=True)]
    dot_general x5 -> x0, matrix products: 95.4 us -> none  [the longest x1 53.5 us: product_pair(): lax.dot_general(left, right_parts[1], dims, preferred_element_type=jnp.fl...]
    unnamed x12 -> x4, local copies, waits for them, and re-layouts: 66.3 us -> 0.01 us
    pallas_call x0 -> x20, Pallas kernels: none -> 54.5 us  [the longest x4 27.4 us: weight_update(): pl.pallas_call(functools.partial(update_kernel, offset, start, height, sl...]
    reduce_scatter x1 -> x0, waiting for transfers between devices: 24.5 us -> none  [body(): shares = lax.psum_scatter(lowered, 'row', scatter_dimension=1, tiled=True)]
    ppermute x0 -> x23, waiting for transfers between devices: none -> 17.2 us  [exchange(): return lax.ppermute(values, axis, [(i, i ^ mask) for i in range(size)])]
    ppermute x0 -> x23, starting transfers between devices: none -> 16.9 us  [exchange(): return lax.ppermute(values, axis, [(i, i ^ mask) for i in range(size)])]
  transfers between devices with their start and end apart: 4 -> 23, of which waited for: 4 -> 8; matrix products, arithmetic and copies ran while one was open for 10% -> 0% of each run, Pallas kernels for 0% -> 48%
where the time goes in v1:
time: 89.8 us; the launch traced here: 89.7 us
  Pallas kernels  54.5 us (61%)
  waiting for transfers between devices  17.2 us (19%)
  starting transfers between devices  16.9 us (19%)
  between operations  0.99 us (1%)
    pallas_call x4, Pallas kernels, weight_update(): pl.pallas_call(functools.partial(update_kernel, offset, start, height, sl...  27.4 us
    ppermute x23, waiting for transfers between devices, exchange(): return lax.ppermute(values, axis, [(i, i ^ mask) for i in range(size)])  17.2 us
    ppermute x23, starting transfers between devices, exchange(): return lax.ppermute(values, axis, [(i, i ^ mask) for i in range(size)])  16.9 us
    pallas_call x4, Pallas kernels, load_weight(): pl.pallas_call(functools.partial(load_kernel, offset, height), out_shape=...  14.4 us
    pallas_call x2, Pallas kernels, adam_chunk(): pl.pallas_call(functools.partial(adam_kernel, n_row, len(pieces), len(mar...  8.37 us
    pallas_call x1, Pallas kernels, lowered_terms(): pl.pallas_call(functools.partial(lowered_kernel, height, cuts), out_shape...  4.18 us
  transfers between devices with their start and end apart: 23, of which 8 were waited for; matrix products, arithmetic and copies ran while one was open for 0% of the time, Pallas kernels for 48%

profile of v1, /device:TPU:0, one launch (start us, length us, event | category | flops | bytes accessed | tf_op | source)
XLA Modules:
  0.0 89.7 jit_solution(14795944588820488323)
XLA Ops:
  0.6 4.2 %lowered_terms.1 = (f32[128,256]{1,0:T(8,128)S(1)}, bf16[128,256]{1,0:T(8,128)(2,1)S(1)}, bf16[128,256]{1,0:T(8,128)(2,1)S(1)}, bf16[128,256]{1,0:T(8,128)(2,1)S...) custom-call(bf16[128,4096]{1,0:T(8,128)(2,1)} %grad_hbm.1, bf16[4096,1024]{1,0:T(8,128)(2,1)} %basis_ref.7, ...), custom_call_target="tpu_custom_call" | custom-call | flops 1 | bytes 1 | tf_op jit(solution)/shard_map/lowered_terms/pallas_call | solution.py:74
  5.3 2.6 %collective-permute-start.1 = (bf16[128,256]{1,0:T(8,128)(2,1)S(1)}, bf16[128,256]{1,0:T(8,128)(2,1)S(1)}, u32[]{:S(2)}, u32[]{:S(2)}) collective-permute-start(bf16[128,256]{1,0:T(8,128)(2,1)S(1)} %get-tuple-element.45), channel_id=1, source_target_pairs={{0,16},{8,24},{16,0},{24,8},{1,17},{9,25},{17,1},{25,9},{2,18},{10... | collective-permute-start | bytes 196616 | tf_op jit(solution)/shard_map/ppermute | solution.py:24
  8.0 2.6 %collective-permute-done.1.refs_2_.refs_3_ = bf16[128,256]{1,0:T(8,128)(2,1)S(1)} collective-permute-done((bf16[128,256]{1,0:T(8,128)(2,1)S(1)}, bf16[128,256]{1,0:T(8,128)(2,1)S(1)}, u32[]{:S(2)}, u32[]{:S(2)}) %collective-permute-start.1) | collective-permute-done | bytes 65568 | tf_op jit(solution)/shard_map/ppermute | solution.py:24
  10.6 1.4 %collective-permute-done.2.refs_3_.refs_4_ = bf16[128,256]{1,0:T(8,128)(2,1)S(1)} collective-permute-done((bf16[128,256]{1,0:T(8,128)(2,1)S(1)}, bf16[128,256]{1,0:T(8,128)(2,1)S(1)}, u32[]{:S(2)}, u32[]{:S(2)}) %collective-permute-start.2) | collective-permute-done | bytes 65568 | tf_op jit(solution)/shard_map/ppermute | solution.py:24
  12.0 1.3 %collective-permute-start.8 = (bf16[256,1024]{1,0:T(8,128)(2,1)S(1)}, bf16[256,1024]{1,0:T(8,128)(2,1)S(1)}, u32[]{:S(2)}, u32[]{:S(2)}) collective-permute-start(bf16[256,1024]{1,0:T(8,128)(2,1)S(1)} %get-tuple-element.53.refs_0_), channel_id=1, source_target_pairs={{0,16},{8,24},{16,0},{24,8},{1,17},{9,25},{17,1},{25,9},{2,18},{10... | collective-permute-start | bytes 1572872 | tf_op jit(solution)/shard_map/ppermute | solution.py:24
  13.3 3.5 %load_weight.4 = (f32[4096,512]{1,0:T(8,128)S(1)}, bf16[16,128]{1,0:T(8,128)(2,1)S(1)}) custom-call(f32[4096,2048]{1,0:T(8,128)} %weight_hbm.7, bf16[128,256]{1,0:T(8,128)(2,1)S(1)} %get-tuple-element.44.mark_in), custom_call_target="tpu_custom_call" | custom-call | flops 1 | bytes 8388608 | tf_op jit(solution)/shard_map/load_weight/pallas_call | solution.py:111
  17.0 1.6 %collective-permute-start.3 = (bf16[256,128]{1,0:T(8,128)(2,1)S(1)}, bf16[256,128]{1,0:T(8,128)(2,1)S(1)}, u32[]{:S(2)}, u32[]{:S(2)}) collective-permute-start(bf16[256,128]{1,0:T(8,128)(2,1)S(1)} %share_sum.1.mark_in.refs_0_), channel_id=1, source_target_pairs={{0,2},{1,3},{2,0},{3,1},{4,6},{5,7},{6,4},{7,5},{8,10},{9,11},{10,... | collective-permute-start | bytes 196616 | tf_op jit(solution)/shard_map/ppermute | solution.py:24
  18.6 2.6 %collective-permute-start.4 = (bf16[256,128]{1,0:T(8,128)(2,1)S(1)}, bf16[256,128]{1,0:T(8,128)(2,1)S(1)}, u32[]{:S(2)}, u32[]{:S(2)}) collective-permute-start(bf16[256,128]{1,0:T(8,128)(2,1)S(1)} %share_sum.1.mark_in.refs_0_), channel_id=1, source_target_pairs={{0,4},{1,5},{2,6},{3,7},{4,0},{5,1},{6,2},{7,3},{8,12},{9,13},{10,... | collective-permute-start | bytes 196616 | tf_op jit(solution)/shard_map/ppermute | solution.py:24
  21.4 3.5 %load_weight.5 = (f32[4096,512]{1,0:T(8,128)S(1)}, bf16[16,128]{1,0:T(8,128)(2,1)S(1)}) custom-call(f32[4096,2048]{1,0:T(8,128)} %weight_hbm.7, bf16[256,128]{1,0:T(8,128)(2,1)S(1)} %share_sum.1.mark_in.refs_0_), custom_call_target="tpu_custom_call" | custom-call | flops 1 | bytes 8388608 | tf_op jit(solution)/shard_map/load_weight/pallas_call | solution.py:111
  25.0 1.1 %collective-permute-done.4.refs_2_ = bf16[256,128]{1,0:T(8,128)(2,1)S(1)} collective-permute-done((bf16[256,128]{1,0:T(8,128)(2,1)S(1)}, bf16[256,128]{1,0:T(8,128)(2,1)S(1)}, u32[]{:S(2)}, u32[]{:S(2)}) %collective-permute-start.4) | collective-permute-done | bytes 65568 | tf_op jit(solution)/shard_map/ppermute | solution.py:24
  26.1 1.3 %collective-permute-done.5.refs_3_ = bf16[256,128]{1,0:T(8,128)(2,1)S(1)} collective-permute-done((bf16[256,128]{1,0:T(8,128)(2,1)S(1)}, bf16[256,128]{1,0:T(8,128)(2,1)S(1)}, u32[]{:S(2)}, u32[]{:S(2)}) %collective-permute-start.5) | collective-permute-done | bytes 65568 | tf_op jit(solution)/shard_map/ppermute | solution.py:24
  28.6 1.5 %collective-permute-start.6 = (bf16[1024,128]{1,0:T(8,128)(2,1)S(1)}, bf16[1024,128]{1,0:T(8,128)(2,1)S(1)}, u32[]{:S(2)}, u32[]{:S(2)}) collective-permute-start(bf16[1024,128]{1,0:T(8,128)(2,1)S(1)} %get-tuple-element.49.refs_0_), channel_id=1, source_target_pairs={{0,1},{1,0},{2,3},{3,2},{4,5},{5,4},{6,7},{7,6},{8,9},{9,8},{10,11... | collective-permute-start | bytes 786440 | tf_op jit(solution)/shard_map/ppermute | solution.py:24
  30.1 3.5 %load_weight.6 = (f32[4096,512]{1,0:T(8,128)S(1)}, bf16[16,128]{1,0:T(8,128)(2,1)S(1)}) custom-call(f32[4096,2048]{1,0:T(8,128)} %weight_hbm.7, bf16[16,128]{1,0:T(8,128)(2,1)S(1)} %get-tuple-element.54.refs_2_.mark_in), custom_call_target="tpu_custom_call" | custom-call | flops 1 | bytes 8388608 | tf_op jit(solution)/shard_map/load_weight/pallas_call | solution.py:111
  33.7 3.0 %collective-permute-done.6.refs_1_ = bf16[1024,128]{1,0:T(8,128)(2,1)S(1)} collective-permute-done((bf16[1024,128]{1,0:T(8,128)(2,1)S(1)}, bf16[1024,128]{1,0:T(8,128)(2,1)S(1)}, u32[]{:S(2)}, u32[]{:S(2)}) %collective-permute-start.6) | collective-permute-done | bytes 262176 | tf_op jit(solution)/shard_map/ppermute | solution.py:24
  36.7 4.2 %adam_chunk.2 = (f32[256,2048]{1,0:T(8,128)}, f32[256,2048]{1,0:T(8,128)}, bf16[256,1024]{1,0:T(8,128)(2,1)S(1)}, bf16[16,128]{1,0:T(8,128)(2,1)S(1)}, bf16[256,...) custom-call(bf16[1024,128]{1,0:T(8,128)(2,1)S(1)} %get-tuple-element.49.refs_0_, ...), custom_call_target="tpu_custom_call" | custom-call | flops 1 | bytes 1 | tf_op jit(solution)/shard_map/adam_chunk/pallas_call | solution.py:228
  43.1 3.8 %load_weight.7 = (f32[4096,512]{1,0:T(8,128)S(1)}, bf16[16,128]{1,0:T(8,128)(2,1)S(1)}) custom-call(f32[4096,2048]{1,0:T(8,128)} %weight_hbm.7, bf16[16,128]{1,0:T(8,128)(2,1)S(1)} %get-tuple-element.58.refs_2_.mark_in), custom_call_target="tpu_custom_call" | custom-call | flops 1 | bytes 8388608 | tf_op jit(solution)/shard_map/load_weight/pallas_call | solution.py:111
  46.9 1.7 %collective-permute-start.16 = (bf16[256,512]{1,0:T(8,128)(2,1)S(1)}, bf16[256,512]{1,0:T(8,128)(2,1)S(1)}, u32[]{:S(2)}, u32[]{:S(2)}) collective-permute-start(bf16[256,512]{1,0:T(8,128)(2,1)S(1)} %get-tuple-element.66.refs_0_), channel_id=1, source_target_pairs={{0,16},{8,24},{16,0},{24,8},{1,17},{9,25},{17,1},{25,9},{2,18},{10... | collective-permute-start | bytes 786440 | tf_op jit(solution)/shard_map/ppermute | solution.py:24
  48.7 4.2 %adam_chunk.3 = (f32[256,2048]{1,0:T(8,128)}, f32[256,2048]{1,0:T(8,128)}, bf16[256,1024]{1,0:T(8,128)(2,1)S(1)}, bf16[16,128]{1,0:T(8,128)(2,1)S(1)}, bf16[256,...) custom-call(bf16[1024,128]{1,0:T(8,128)(2,1)S(1)} %get-tuple-element.49.refs_0_, ...), custom_call_target="tpu_custom_call", output_to_operand_aliasing={{0}: (9, {}), {1}: (10, {})} | custom-call | flops 1 | bytes 1 | tf_op jit(solution)/shard_map/adam_chunk/pallas_call | solution.py:228
  53.8 3.3 %collective-permute-done.16.refs_0_ = bf16[256,512]{1,0:T(8,128)(2,1)S(1)} collective-permute-done((bf16[256,512]{1,0:T(8,128)(2,1)S(1)}, bf16[256,512]{1,0:T(8,128)(2,1)S(1)}, u32[]{:S(2)}, u32[]{:S(2)}) %collective-permute-start.16) | collective-permute-done | bytes 262176 | tf_op jit(solution)/shard_map/ppermute | solution.py:24
  58.0 6.5 %weight_update.4 = (f32[4096,2048]{1,0:T(8,128)}, bf16[16,128]{1,0:T(8,128)(2,1)S(1)}) custom-call(bf16[4096,1024]{1,0:T(8,128)(2,1)S(1)} %bitcast.1, bf16[256,512]{1,0:T(8,128)(2,1)S(1)} %get-tuple-element.70.refs_0_, bf16[256,1024]{1,0:T(8,128)(2,1)S(1)} %collective-permute-done.15.refs_1_, bf16[256,512]{1,0:T(8,128)(2,1)S(1)} %after.11.refs_2_, ...), custom_call_target="tpu_custom_call" | custom-call | flops 4294967296 | bytes 8388608 | tf_op jit(solution)/shard_map/weight_update/pallas_call | solution.py:286
  64.5 3.5 %collective-permute-done.21.refs_0_ = bf16[256,512]{1,0:T(8,128)(2,1)S(1)} collective-permute-done((bf16[256,512]{1,0:T(8,128)(2,1)S(1)}, bf16[256,512]{1,0:T(8,128)(2,1)S(1)}, u32[]{:S(2)}, u32[]{:S(2)}) %collective-permute-start.21) | collective-permute-done | bytes 262176 | tf_op jit(solution)/shard_map/ppermute | solution.py:24
  68.0 6.7 %weight_update.5 = (f32[4096,2048]{1,0:T(8,128)}, bf16[16,128]{1,0:T(8,128)(2,1)S(1)}) custom-call(bf16[4096,1024]{1,0:T(8,128)(2,1)S(1)} %bitcast.1, bf16[256,512]{1,0:T(8,128)(2,1)S(1)} %get-tuple-element.66.refs_0_, bf16[256,1024]{1,0:T(8,128)(2,1)S(1)} %collective-permute-done.15.refs_1_, ...), custom_call_target="tpu_custom_call", output_to_operand_aliasing={{0}: (6, {})} | custom-call | flops 4294967296 | bytes 8388608 | tf_op jit(solution)/shard_map/weight_update/pallas_call | solution.py:286
  75.3 7.1 %weight_update.6 = (f32[4096,2048]{1,0:T(8,128)}, bf16[16,128]{1,0:T(8,128)(2,1)}) custom-call(bf16[4096,1024]{1,0:T(8,128)(2,1)S(1)} %bitcast.1, bf16[256,512]{1,0:T(8,128)(2,1)S(1)} %get-tuple-element.75.refs_0_, bf16[256,1024]{1,0:T(8,128)(2,1)S(1)} %collective-permute-done.13.refs_1_, ...), custom_call_target="tpu_custom_call", output_to_operand_aliasing={{0}: (6, {})} | custom-call | flops 4294967296 | bytes 8388608 | tf_op jit(solution)/shard_map/weight_update/pallas_call | solution.py:286
  82.4 7.1 %weight_update.7 = (f32[4096,2048]{1,0:T(8,128)}, bf16[16,128]{1,0:T(8,128)(2,1)}) custom-call(bf16[4096,1024]{1,0:T(8,128)(2,1)S(1)} %bitcast.1, bf16[256,512]{1,0:T(8,128)(2,1)S(1)} %get-tuple-element.64.refs_0_, bf16[256,1024]{1,0:T(8,128)(2,1)S(1)} %collective-permute-done.13.refs_1_, ...), custom_call_target="tpu_custom_call", output_to_operand_aliasing={{0}: (6, {})} | custom-call | flops 4294967296 | bytes 8388608 | tf_op jit(solution)/shard_map/weight_update/pallas_call | solution.py:286
  (47 shorter events, 6.8 us)
Async XLA Ops:
  4.8 3.2 %collective-permute-start = (bf16[128,256]{1,0:T(8,128)(2,1)S(1)}, bf16[128,256]{1,0:T(8,128)(2,1)S(1)}, u32[]{:S(2)}, u32[]{:S(2)}) collective-permute-start(bf16[128,256]{1,0:T(8,128)(2,1)S(1)} %get-tuple-element.44.mark_in), channel_id=1, source_target_pairs={{0,8},{8,0},{16,24},{24,16},{1,9},{9,1},{17,25},{25,17},{2,10},{10... | collective-permute-start | bytes 196616 | tf_op jit(solution)/shard_map/ppermute | solution.py:24
  5.3 5.3 %collective-permute-start.1 = (bf16[128,256]{1,0:T(8,128)(2,1)S(1)}, bf16[128,256]{1,0:T(8,128)(2,1)S(1)}, u32[]{:S(2)}, u32[]{:S(2)}) collective-permute-start(bf16[128,256]{1,0:T(8,128)(2,1)S(1)} %get-tuple-element.45), channel_id=1, source_target_pairs={{0,16},{8,24},{16,0},{24,8},{1,17},{9,25},{17,1},{25,9},{2,18},{10... | collective-permute-start | bytes 196616 | tf_op jit(solution)/shard_map/ppermute | solution.py:24
  7.9 4.0 %collective-permute-start.2 = (bf16[128,256]{1,0:T(8,128)(2,1)S(1)}, bf16[128,256]{1,0:T(8,128)(2,1)S(1)}, u32[]{:S(2)}, u32[]{:S(2)}) collective-permute-start(bf16[128,256]{1,0:T(8,128)(2,1)S(1)} %get-tuple-element.46), channel_id=1, source_target_pairs={{0,24},{8,16},{16,8},{24,0},{1,25},{9,17},{17,9},{25,1},{2,26},{10... | collective-permute-start | bytes 196616 | tf_op jit(solution)/shard_map/ppermute | solution.py:24
  12.0 15.4 %collective-permute-start.8 = (bf16[256,1024]{1,0:T(8,128)(2,1)S(1)}, bf16[256,1024]{1,0:T(8,128)(2,1)S(1)}, u32[]{:S(2)}, u32[]{:S(2)}) collective-permute-start(bf16[256,1024]{1,0:T(8,128)(2,1)S(1)} %get-tuple-element.53.refs_0_), channel_id=1, source_target_pairs={{0,16},{8,24},{16,0},{24,8},{1,17},{9,25},{17,1},{25,9},{2,18},{10... | collective-permute-start | bytes 1572872 | tf_op jit(solution)/shard_map/ppermute | solution.py:24
  17.0 8.0 %collective-permute-start.3 = (bf16[256,128]{1,0:T(8,128)(2,1)S(1)}, bf16[256,128]{1,0:T(8,128)(2,1)S(1)}, u32[]{:S(2)}, u32[]{:S(2)}) collective-permute-start(bf16[256,128]{1,0:T(8,128)(2,1)S(1)} %share_sum.1.mark_in.refs_0_), channel_id=1, source_target_pairs={{0,2},{1,3},{2,0},{3,1},{4,6},{5,7},{6,4},{7,5},{8,10},{9,11},{10,... | collective-permute-start | bytes 196616 | tf_op jit(solution)/shard_map/ppermute | solution.py:24
  18.6 7.5 %collective-permute-start.4 = (bf16[256,128]{1,0:T(8,128)(2,1)S(1)}, bf16[256,128]{1,0:T(8,128)(2,1)S(1)}, u32[]{:S(2)}, u32[]{:S(2)}) collective-permute-start(bf16[256,128]{1,0:T(8,128)(2,1)S(1)} %share_sum.1.mark_in.refs_0_), channel_id=1, source_target_pairs={{0,4},{1,5},{2,6},{3,7},{4,0},{5,1},{6,2},{7,3},{8,12},{9,13},{10,... | collective-permute-start | bytes 196616 | tf_op jit(solution)/shard_map/ppermute | solution.py:24
  21.2 6.2 %collective-permute-start.5 = (bf16[256,128]{1,0:T(8,128)(2,1)S(1)}, bf16[256,128]{1,0:T(8,128)(2,1)S(1)}, u32[]{:S(2)}, u32[]{:S(2)}) collective-permute-start(bf16[256,128]{1,0:T(8,128)(2,1)S(1)} %share_sum.1.mark_in.refs_0_), channel_id=1, source_target_pairs={{0,6},{1,7},{2,4},{3,5},{4,2},{5,3},{6,0},{7,1},{8,14},{9,15},{10,... | collective-permute-start | bytes 196616 | tf_op jit(solution)/shard_map/ppermute | solution.py:24
  27.4 9.2 %collective-permute-start.9 = (bf16[256,1024]{1,0:T(8,128)(2,1)S(1)}, bf16[256,1024]{1,0:T(8,128)(2,1)S(1)}, u32[]{:S(2)}, u32[]{:S(2)}) collective-permute-start(bf16[256,1024]{1,0:T(8,128)(2,1)S(1)} %get-tuple-element.55.refs_2_), channel_id=1, source_target_pairs={{0,8},{8,0},{16,24},{24,16},{1,9},{9,1},{17,25},{25,17},{2,10},{10... | collective-permute-start | bytes 1572872 | tf_op jit(solution)/shard_map/ppermute | solution.py:24
  27.5 9.2 %collective-permute-start.10 = (bf16[256,1024]{1,0:T(8,128)(2,1)S(1)}, bf16[256,1024]{1,0:T(8,128)(2,1)S(1)}, u32[]{:S(2)}, u32[]{:S(2)}) collective-permute-start(bf16[256,1024]{1,0:T(8,128)(2,1)S(1)} %get-tuple-element.56.refs_4_), channel_id=1, source_target_pairs={{0,8},{8,0},{16,24},{24,16},{1,9},{9,1},{17,25},{25,17},{2,10},{10... | collective-permute-start | bytes 1572872 | tf_op jit(solution)/shard_map/ppermute | solution.py:24
  28.0 13.9 %collective-permute-start.7 = (bf16[256,1024]{1,0:T(8,128)(2,1)S(1)}, bf16[256,1024]{1,0:T(8,128)(2,1)S(1)}, u32[]{:S(2)}, u32[]{:S(2)}) collective-permute-start(bf16[256,1024]{1,0:T(8,128)(2,1)S(1)} %get-tuple-element.52.refs_0_), channel_id=1, source_target_pairs={{0,16},{8,24},{16,0},{24,8},{1,17},{9,25},{17,1},{25,9},{2,18},{10... | collective-permute-start | bytes 1572872 | tf_op jit(solution)/shard_map/ppermute | solution.py:24
  28.6 8.0 %collective-permute-start.6 = (bf16[1024,128]{1,0:T(8,128)(2,1)S(1)}, bf16[1024,128]{1,0:T(8,128)(2,1)S(1)}, u32[]{:S(2)}, u32[]{:S(2)}) collective-permute-start(bf16[1024,128]{1,0:T(8,128)(2,1)S(1)} %get-tuple-element.49.refs_0_), channel_id=1, source_target_pairs={{0,1},{1,0},{2,3},{3,2},{4,5},{5,4},{6,7},{7,6},{8,9},{9,8},{10,11... | collective-permute-start | bytes 786440 | tf_op jit(solution)/shard_map/ppermute | solution.py:24
  41.9 6.8 %collective-permute-start.11 = (bf16[256,1024]{1,0:T(8,128)(2,1)S(1)}, bf16[256,1024]{1,0:T(8,128)(2,1)S(1)}, u32[]{:S(2)}, u32[]{:S(2)}) collective-permute-start(bf16[256,1024]{1,0:T(8,128)(2,1)S(1)} %get-tuple-element.59.refs_2_), channel_id=1, source_target_pairs={{0,8},{8,0},{16,24},{24,16},{1,9},{9,1},{17,25},{25,17},{2,10},{10... | collective-permute-start | bytes 1572872 | tf_op jit(solution)/shard_map/ppermute | solution.py:24
  41.9 6.8 %collective-permute-start.12 = (bf16[256,1024]{1,0:T(8,128)(2,1)S(1)}, bf16[256,1024]{1,0:T(8,128)(2,1)S(1)}, u32[]{:S(2)}, u32[]{:S(2)}) collective-permute-start(bf16[256,1024]{1,0:T(8,128)(2,1)S(1)} %get-tuple-element.60.refs_4_), channel_id=1, source_target_pairs={{0,8},{8,0},{16,24},{24,16},{1,9},{9,1},{17,25},{25,17},{2,10},{10... | collective-permute-start | bytes 1572872 | tf_op jit(solution)/shard_map/ppermute | solution.py:24
  42.4 14.7 %collective-permute-start.15 = (bf16[256,1024]{1,0:T(8,128)(2,1)S(1)}, bf16[256,1024]{1,0:T(8,128)(2,1)S(1)}, u32[]{:S(2)}, u32[]{:S(2)}) collective-permute-start(bf16[256,1024]{1,0:T(8,128)(2,1)S(1)} %get-tuple-element.67), channel_id=1, source_target_pairs={{0,8},{8,0},{16,24},{24,16},{1,9},{9,1},{17,25},{25,17},{2,10},{10... | collective-permute-start | bytes 1572872 | tf_op jit(solution)/shard_map/ppermute | solution.py:24
  42.4 15.6 %slice-start.1 = ((s8[8388608]{0:T(1024)(128)(4,1)}), s8[4194304]{0:T(1024)(128)(4,1)S(1)}, s32[]{:S(2)}) async-start(s8[8388608]{0:T(1024)(128)(4,1)} %bitcast), calls=%async_computation.1 | async-start | bytes 8388608
  42.4 10.5 %collective-permute-start.18 = (bf16[256,512]{1,0:T(8,128)(2,1)S(1)}, bf16[256,512]{1,0:T(8,128)(2,1)S(1)}, u32[]{:S(2)}, u32[]{:S(2)}) collective-permute-start(bf16[256,512]{1,0:T(8,128)(2,1)S(1)} %get-tuple-element.70.refs_0_), channel_id=1, source_target_pairs={{0,16},{8,24},{16,0},{24,8},{1,17},{9,25},{17,1},{25,9},{2,18},{10... | collective-permute-start | bytes 786440 | tf_op jit(solution)/shard_map/ppermute | solution.py:24
  46.9 10.2 %collective-permute-start.16 = (bf16[256,512]{1,0:T(8,128)(2,1)S(1)}, bf16[256,512]{1,0:T(8,128)(2,1)S(1)}, u32[]{:S(2)}, u32[]{:S(2)}) collective-permute-start(bf16[256,512]{1,0:T(8,128)(2,1)S(1)} %get-tuple-element.66.refs_0_), channel_id=1, source_target_pairs={{0,16},{8,24},{16,0},{24,8},{1,17},{9,25},{17,1},{25,9},{2,18},{10... | collective-permute-start | bytes 786440 | tf_op jit(solution)/shard_map/ppermute | solution.py:24
  52.9 5.1 %collective-permute-start.19 = (bf16[256,512]{1,0:T(8,128)(2,1)S(1)}, bf16[256,512]{1,0:T(8,128)(2,1)S(1)}, u32[]{:S(2)}, u32[]{:S(2)}) collective-permute-start(bf16[256,512]{1,0:T(8,128)(2,1)S(1)} %after.11.refs_2_), channel_id=1, source_target_pairs={{0,8},{8,0},{16,24},{24,16},{1,9},{9,1},{17,25},{25,17},{2,10},{10... | collective-permute-start | bytes 786440 | tf_op jit(solution)/shard_map/ppermute | solution.py:24
  53.0 22.3 %collective-permute-start.13 = (bf16[256,1024]{1,0:T(8,128)(2,1)S(1)}, bf16[256,1024]{1,0:T(8,128)(2,1)S(1)}, u32[]{:S(2)}, u32[]{:S(2)}) collective-permute-start(bf16[256,1024]{1,0:T(8,128)(2,1)S(1)} %get-tuple-element.65), channel_id=1, source_target_pairs={{0,8},{8,0},{16,24},{24,16},{1,9},{9,1},{17,25},{25,17},{2,10},{10... | collective-permute-start | bytes 1572872 | tf_op jit(solution)/shard_map/ppermute | solution.py:24
  53.5 21.2 %collective-permute-start.14 = (bf16[256,512]{1,0:T(8,128)(2,1)S(1)}, bf16[256,512]{1,0:T(8,128)(2,1)S(1)}, u32[]{:S(2)}, u32[]{:S(2)}) collective-permute-start(bf16[256,512]{1,0:T(8,128)(2,1)S(1)} %get-tuple-element.64.refs_0_), channel_id=1, source_target_pairs={{0,16},{8,24},{16,0},{24,8},{1,17},{9,25},{17,1},{25,9},{2,18},{10... | collective-permute-start | bytes 786440 | tf_op jit(solution)/shard_map/ppermute | solution.py:24
  57.1 10.9 %collective-permute-start.17 = (bf16[256,512]{1,0:T(8,128)(2,1)S(1)}, bf16[256,512]{1,0:T(8,128)(2,1)S(1)}, u32[]{:S(2)}, u32[]{:S(2)}) collective-permute-start(bf16[256,512]{1,0:T(8,128)(2,1)S(1)} %after.10.refs_2_), channel_id=1, source_target_pairs={{0,8},{8,0},{16,24},{24,16},{1,9},{9,1},{17,25},{25,17},{2,10},{10... | collective-permute-start | bytes 786440 | tf_op jit(solution)/shard_map/ppermute | solution.py:24
  57.1 10.8 %collective-permute-start.21 = (bf16[256,512]{1,0:T(8,128)(2,1)S(1)}, bf16[256,512]{1,0:T(8,128)(2,1)S(1)}, u32[]{:S(2)}, u32[]{:S(2)}) collective-permute-start(bf16[256,512]{1,0:T(8,128)(2,1)S(1)} %get-tuple-element.75.refs_0_), channel_id=1, source_target_pairs={{0,16},{8,24},{16,0},{24,8},{1,17},{9,25},{17,1},{25,9},{2,18},{10... | collective-permute-start | bytes 786440 | tf_op jit(solution)/shard_map/ppermute | solution.py:24
  68.0 7.3 %collective-permute-start.22 = (bf16[256,512]{1,0:T(8,128)(2,1)S(1)}, bf16[256,512]{1,0:T(8,128)(2,1)S(1)}, u32[]{:S(2)}, u32[]{:S(2)}) collective-permute-start(bf16[256,512]{1,0:T(8,128)(2,1)S(1)} %after.13.refs_2_), channel_id=1, source_target_pairs={{0,8},{8,0},{16,24},{24,16},{1,9},{9,1},{17,25},{25,17},{2,10},{10... | collective-permute-start | bytes 786440 | tf_op jit(solution)/shard_map/ppermute | solution.py:24
  74.7 7.7 %collective-permute-start.20 = (bf16[256,512]{1,0:T(8,128)(2,1)S(1)}, bf16[256,512]{1,0:T(8,128)(2,1)S(1)}, u32[]{:S(2)}, u32[]{:S(2)}) collective-permute-start(bf16[256,512]{1,0:T(8,128)(2,1)S(1)} %after.12.refs_2_), channel_id=1, source_target_pairs={{0,8},{8,0},{16,24},{24,16},{1,9},{9,1},{17,25},{25,17},{2,10},{10... | collective-permute-start | bytes 786440 | tf_op jit(solution)/shard_map/ppermute | solution.py:24
  (1 other events, 15.6 us)

commit v2 on v1

v2 whole, which is shorter than its diff:
```python
import functools

import jax
import jax.numpy as jnp
from jax import lax
from jax.experimental import pallas as pl
from jax.experimental.pallas import tpu as pltpu
from jax.sharding import PartitionSpec as P

STEP = 10

first_decay = 0.9
second_decay = 0.99
adam_epsilon = 1e-08
learn_rate = 4.0

MIB = 1 << 20
VMEM = pl.BlockSpec(memory_space=pltpu.VMEM)
ANY = pl.BlockSpec(memory_space=pltpu.HBM)
MARK = jax.ShapeDtypeStruct((16, 128), jnp.bfloat16)


def exchange(values, axis, size, mask):
    return lax.ppermute(values, axis, [(i, i ^ mask) for i in range(size)])


def parameters(mib):
    return pltpu.CompilerParams(vmem_limit_bytes=mib * MIB)


def cost(flops, moved):
    return pl.CostEstimate(flops=flops, bytes_accessed=moved, transcendentals=0)


def lowered_kernel(height, cuts, grad_hbm, basis_hbm, input_hbm, *refs):
    n_cuts = len(cuts)
    out_refs, whole_ref, input_refs = refs[: -n_cuts - 5], refs[-n_cuts - 5], refs[-n_cuts - 4 : -4]
    grad_ref, basis_ref, total_ref, sems = refs[-4:]
    me = lax.axis_index("row")
    count = basis_ref.shape[0] // height

    def rows(step):
        return slice(step * height, (step + 1) * height)

    copies = [pltpu.make_async_copy(grad_hbm, grad_ref, sems.at[0])]
    for step in range(count):
        copies.append(pltpu.make_async_copy(basis_hbm.at[rows(step)], basis_ref.at[rows(step)], sems.at[1 + step]))
    for index, (at, width) in enumerate(cuts):
        here = slice(at, at + width)
        copies.append(pltpu.make_async_copy(input_hbm.at[:, here], input_refs[index], sems.at[1 + count + index]))
    copies.append(pltpu.make_async_copy(input_hbm, whole_ref, sems.at[1 + count + n_cuts]))
    for copy in copies:
        copy.start()
    copies[0].wait()
    for step in range(count):
        copies[1 + step].wait()
        term = jnp.dot(grad_ref[:, rows(step)], basis_ref[rows(step), :], preferred_element_type=jnp.float32)
        if step == 0:
            total_ref[...] = term
        else:
            total_ref[...] += term
    width = out_refs[0].shape[1]
    for mask, out_ref in enumerate(out_refs):
        columns = pl.ds(pl.multiple_of((me ^ mask) * width, width), width)
        out_ref[...] = total_ref[:, columns].astype(out_ref.dtype)
    for copy in copies[1 + count :]:
        copy.wait()


def lowered_terms(grad_out, projector, activations, cuts, n_row):
    tokens, ranks = grad_out.shape[0], projector.shape[1] // n_row
    height = min(512, projector.shape[0])
    count = projector.shape[0] // height
    kinds = [jnp.float32] + [jnp.bfloat16] * (n_row - 1)
    results = pl.pallas_call(
        functools.partial(lowered_kernel, height, cuts),
        out_shape=[jax.ShapeDtypeStruct((tokens, ranks), kind) for kind in kinds]
        + [pltpu.VMEM((activations.shape[0], width), activations.dtype) for _, width in [(0, activations.shape[1])] + cuts],
        in_specs=[ANY] * 3,
        out_specs=[VMEM] * (n_row + 1 + len(cuts)),
        scratch_shapes=[
            pltpu.VMEM(grad_out.shape, grad_out.dtype),
            pltpu.VMEM(projector.shape, projector.dtype),
            pltpu.VMEM((tokens, projector.shape[1]), jnp.float32),
            pltpu.SemaphoreType.DMA((2 + count + len(cuts),)),
        ],
        compiler_params=parameters(14),
        cost_estimate=cost(1, 1),
        name="lowered_terms",
    )(grad_out, projector, activations)
    return results[:n_row], results[n_row], results[n_row + 1 :]


def load_kernel(cuts, height, weight_hbm, mark_in, *refs):
    del mark_in
    held_refs, mark_ref, sems = refs[:-2], refs[-2], refs[-1]
    copies = []
    for index, (at, width) in enumerate(cuts):
        for step in range(weight_hbm.shape[0] // height):
            rows = slice(step * height, (step + 1) * height)
            source = weight_hbm.at[rows, at : at + width]
            copies.append(pltpu.make_async_copy(source, held_refs[index].at[rows], sems.at[index, step]))
    for copy in copies:
        copy.start()
    mark_ref[...] = jnp.zeros_like(mark_ref)
    for copy in copies:
        copy.wait()


def load_weight(weight, cuts, mark):
    rows = weight.shape[0]
    height = min(1024, rows)
    return pl.pallas_call(
        functools.partial(load_kernel, cuts, height),
        out_shape=[pltpu.VMEM((rows, width), weight.dtype) for _, width in cuts] + [MARK],
        in_specs=[ANY, VMEM],
        out_specs=[VMEM] * (len(cuts) + 1),
        scratch_shapes=[pltpu.SemaphoreType.DMA((len(cuts), rows // height))],
        compiler_params=parameters(2),
        cost_estimate=cost(1, 1),
        name="load_weight",
    )(weight, mark)


def share_kernel(n_terms, *refs):
    total = refs[0][...]
    for ref in refs[1:n_terms]:
        total = total + ref[...].astype(jnp.float32)
    refs[-1][...] = total.T.astype(jnp.bfloat16)


def share_sum(terms, marks):
    tokens, ranks = terms[0].shape
    return pl.pallas_call(
        functools.partial(share_kernel, len(terms)),
        out_shape=jax.ShapeDtypeStruct((ranks, tokens), jnp.bfloat16),
        in_specs=[VMEM] * (len(terms) + len(marks)),
        out_specs=VMEM,
        compiler_params=parameters(4),
        cost_estimate=cost(1, 1),
        name="share_sum",
    )(*terms, *marks)


def stack_kernel(n_parts, *refs):
    out_ref, mark_ref = refs[-2:]
    height = refs[0].shape[0]
    for index, part in enumerate(refs[:n_parts]):
        out_ref[index * height : (index + 1) * height] = part[...]
    mark_ref[...] = jnp.zeros_like(mark_ref)


def stack(parts, marks):
    height, width = parts[0].shape
    return pl.pallas_call(
        functools.partial(stack_kernel, len(parts)),
        out_shape=[jax.ShapeDtypeStruct((height * len(parts), width), parts[0].dtype), MARK],
        in_specs=[VMEM] * (len(parts) + len(marks)),
        out_specs=[VMEM, VMEM],
        compiler_params=parameters(4),
        cost_estimate=cost(1, 1),
        name="stack",
    )(*parts, *marks)


def adam_kernel(counts, n_pieces, n_skip, offset, step, cuts, *refs):
    pieces, refs = refs[:n_pieces], refs[n_pieces:]
    inputs = []
    for count in counts:
        inputs.append(refs[:count])
        refs = refs[count:]
    first_ref, second_ref, refs = refs[0], refs[1], refs[2 + n_skip :]
    new_first_ref, new_second_ref, direction_ref, mark_ref = refs[:4]
    part_refs, (lowered_ref, firsts, seconds, sems) = refs[4:-4], refs[-4:]
    mark_ref[...] = jnp.zeros_like(mark_ref)
    depth, width = inputs[0][0].shape
    row, col = lax.axis_index("row"), lax.axis_index("col")
    ranks, span = lowered_ref.shape[0], pieces[0].shape[1]
    if n_pieces > 1:
        for mask in range(lowered_ref.shape[1] // span):
            columns = pl.ds(pl.multiple_of((col ^ mask) * span, span), span)
            held = pieces[mask % 2]
            lowered_ref[:, columns] = held[mask // 2 * ranks : (mask // 2 + 1) * ranks, :]
    else:
        lowered_ref[...] = pieces[0][...]
    copies = []
    for number, at in enumerate(range(0, width, step)):
        here = slice(at, at + step)
        there = slice(offset + at, offset + at + step)
        lowgrad = None
        for mask, blocks in enumerate(inputs):
            columns = pl.ds(pl.multiple_of((row ^ mask) * depth, depth), depth)
            span = blocks[0].shape[1]
            begin = (offset + at if mask == 1 else at) % span
            block = blocks[0 if mask == 1 else at // span][:, begin : begin + step]
            term = jnp.dot(lowered_ref[:, columns], block, preferred_element_type=jnp.float32)
            lowgrad = term if lowgrad is None else lowgrad + term
        new_first = first_decay * first_ref[:, there] + (1.0 - first_decay) * lowgrad
        new_second = second_decay * second_ref[:, there] + (1.0 - second_decay) * lowgrad * lowgrad
        firsts[number] = new_first
        seconds[number] = new_second
        for which, (source, target) in enumerate(((firsts, new_first_ref), (seconds, new_second_ref))):
            copy = pltpu.make_async_copy(source.at[number], target.at[:, there], sems.at[number, which])
            copy.start()
            copies.append(copy)
        corrected_first = new_first / (1.0 - first_decay**STEP)
        corrected_second = new_second / (1.0 - second_decay**STEP)
        direction = corrected_first / (jnp.sqrt(corrected_second) + adam_epsilon)
        direction_ref[:, here] = (learn_rate * direction).astype(direction_ref.dtype)
    for (at, width), part_ref in zip(cuts, part_refs):
        part_ref[...] = direction_ref[:, at : at + width]
    for copy in copies:
        copy.wait()


def adam_chunk(pieces, inputs, first, second, marks, carried, offset, cuts, n_row):
    ranks = first.shape[0]
    depth, width = inputs[0][0].shape
    tokens = depth * n_row
    counts = [len(blocks) for blocks in inputs]
    step = min(256, width)
    count = width // step
    n_plain = len(pieces) + sum(counts) + 2 + len(marks)
    return pl.pallas_call(
        functools.partial(adam_kernel, counts, len(pieces), len(marks) + len(carried), offset, step, cuts),
        out_shape=[
            jax.ShapeDtypeStruct(first.shape, jnp.float32),
            jax.ShapeDtypeStruct(first.shape, jnp.float32),
            jax.ShapeDtypeStruct((ranks, width), jnp.bfloat16),
            MARK,
            *(jax.ShapeDtypeStruct((ranks, part), jnp.bfloat16) for _, part in cuts),
        ],
        in_specs=[VMEM] * n_plain + [ANY] * len(carried),
        out_specs=[ANY, ANY, VMEM, VMEM] + [VMEM] * len(cuts),
        scratch_shapes=[
            pltpu.VMEM((ranks, tokens), jnp.bfloat16),
            pltpu.VMEM((count, ranks, step), jnp.float32),
            pltpu.VMEM((count, ranks, step), jnp.float32),
            pltpu.SemaphoreType.DMA((count, 2)),
        ],
        input_output_aliases={n_plain: 0, n_plain + 1: 1} if carried else {},
        compiler_params=parameters(6),
        cost_estimate=cost(1, 1),
        name="adam_chunk",
    )(*pieces, *sum(inputs, []), first, second, *marks, *carried)


def gather_pair(pair, parts, start):
    core = lax.rem(lax.axis_index("row"), 2)
    width = pair.shape[1]
    ranks = parts[0][0].shape[0]
    for mask, pieces in enumerate(parts):
        rows = pl.ds(pl.multiple_of((core ^ mask) * ranks, ranks), ranks)
        span = min(width, pieces[0].shape[1])
        for index, piece in enumerate(pieces):
            pair[rows, index * span : (index + 1) * span] = piece[:, start : start + span]


def update_kernel(far_at, start, height, far_counts, n_near, n_far_held, n_near_held, n_skip, basis_ref, *refs):
    far_parts = []
    for count in far_counts:
        far_parts.append(refs[:count])
        refs = refs[count:]
    near_parts = [[part] for part in refs[:n_near]]
    n_held = n_far_held + n_near_held
    refs = refs[n_near + n_held + n_skip :]
    outs, held_refs = refs[: len(refs) - n_held - 3], refs[-n_held - 3 : -3]
    mark_ref, pairs, sems = refs[-3:]
    span = held_refs[0].shape[1]
    count = held_refs[0].shape[0] // height
    ranks = pairs.shape[1] // 2
    chip = lax.axis_index("row") // 2

    def subtract(rows, helds, mask, pair):
        taken = pl.ds(pl.multiple_of((chip ^ mask) * 2 * ranks, 2 * ranks), 2 * ranks)
        update = jnp.dot(basis_ref[rows, taken], pair, preferred_element_type=jnp.float32)
        for index, held in enumerate(helds):
            held[rows, :] = held[rows, :] - update[:, index * span : (index + 1) * span]

    copies = []
    for index in range(0, len(far_parts), 2):
        gather_pair(pairs.at[index // 2 + 1], far_parts[index : index + 2], 0)
    if n_near:
        gather_pair(pairs.at[0], near_parts, start)
    for step in range(count if far_parts else 0):
        rows = slice(step * height, (step + 1) * height)
        for index in range(0, len(far_parts), 2):
            subtract(rows, held_refs[:n_far_held], index // 2 + 1, pairs[index // 2 + 1])
        for index, held in enumerate(held_refs[:n_far_held]):
            target = outs[0].at[rows, far_at + index * span : far_at + (index + 1) * span]
            copies.append(pltpu.make_async_copy(held.at[rows], target, sems.at[step, index]))
            copies[-1].start()
    for step in range(count if n_near else 0):
        rows = slice(step * height, (step + 1) * height)
        subtract(rows, held_refs[n_far_held:], 0, pairs[0])
    mark_ref[...] = jnp.zeros_like(mark_ref)
    for copy in copies:
        copy.wait()


def weight_update(projector, shape, marks, far=(), far_held=(), far_at=0, near=(), near_held=(), start=0, carried=()):
    helds = [*far_held, *near_held]
    counts = [len(pieces) for pieces in far]
    flat = sum(far, []) + list(near)
    rows, span = helds[0].shape
    ranks, width = flat[0].shape[0], span * max(len(far_held), len(near_held))
    height = min(512, rows)
    n_plain = 1 + len(flat)
    out_shape = [jax.ShapeDtypeStruct(shape, jnp.float32)] if far else []
    aliases = {n_plain + index: len(out_shape) + index for index in range(len(helds))}
    if carried:
        aliases[n_plain + len(helds) + len(marks)] = 0
    n_skip = len(marks) + len(carried)
    return pl.pallas_call(
        functools.partial(
            update_kernel, far_at, start, height, counts, len(near), len(far_held), len(near_held), n_skip
        ),
        out_shape=out_shape + [pltpu.VMEM(held.shape, jnp.float32) for held in helds] + [MARK],
        in_specs=[VMEM] * (n_plain + len(helds) + len(marks)) + [ANY] * len(carried),
        out_specs=[ANY] * len(out_shape) + [VMEM] * (len(helds) + 1),
        scratch_shapes=[
            pltpu.VMEM((1 + len(far) // 2, 2 * ranks, width), jnp.bfloat16),
            pltpu.SemaphoreType.DMA((rows // height, max(1, len(far_held)))),
        ],
        input_output_aliases=aliases,
        compiler_params=parameters(6),
        cost_estimate=cost(1, 1),
        name="weight_update",
    )(projector, *flat, *helds, *marks, *carried)


def after_kernel(cuts, n_marks, *refs):
    n_parts = (len(refs) - n_marks) // (2 + len(cuts))
    pieces = refs[2 * n_parts + n_marks :]
    for index in range(n_parts):
        for number, (at, width) in enumerate(cuts):
            pieces[index * len(cuts) + number][...] = refs[index][:, at : at + width]


def after(parts, *marks, cuts=()):
    shapes = [jax.ShapeDtypeStruct(part.shape, part.dtype) for part in parts]
    for part in parts:
        shapes += [jax.ShapeDtypeStruct((part.shape[0], width), part.dtype) for _, width in cuts]
    results = pl.pallas_call(
        functools.partial(after_kernel, cuts, len(marks)),
        out_shape=shapes,
        in_specs=[VMEM] * (len(parts) + len(marks)),
        out_specs=[VMEM] * len(shapes),
        input_output_aliases={i: i for i in range(len(parts))},
        compiler_params=parameters(2),
        cost_estimate=cost(1, 1),
        name="after",
    )(*parts, *marks)
    return results[: len(parts)], results[len(parts) :]


def over_y(values, n_row):
    return [exchange(values, "row", n_row, mask) for mask in range(2, n_row, 2)]


def with_core(far, marks, n_row, pieces):
    cuts = cut(far[0].shape[1], (1,) * pieces)
    far, chunks = after(far, *marks, cuts=cuts)
    parts = []
    for index, part in enumerate(far):
        sent = chunks[index * len(cuts) : (index + 1) * len(cuts)]
        parts += [[part], [exchange(piece, "row", n_row, 1) for piece in sent]]
    return parts


def cut(total, parts):
    unit = total // sum(parts)
    if unit % 128:
        return [(0, total)]
    return [(sum(parts[:index]) * unit, part * unit) for index, part in enumerate(parts)]


def body(n_row, n_col, grad_out, activations, projector, weight, first_moment, second_moment):
    grad_out, activations, weight = [
        pltpu.with_memory_space_constraint(values, pltpu.HBM)
        for values in (grad_out, activations, weight)
    ]
    total = activations.shape[1]
    halves = cut(total, (1, 1))
    parts_of = [cut(width, (1, 1)) for _, width in halves]
    strips = cut(total, (1,) * 8)
    loads = [strips[6:], strips[3:6], strips[:3]]
    held = []

    def load(mark):
        cuts = loads.pop(0)
        if not cuts:
            return []
        *chunks, mark = load_weight(weight, cuts, mark)
        held[:0] = chunks
        return [mark]

    basis = pltpu.with_memory_space_constraint(projector, pltpu.HBM)
    terms, whole, inputs = lowered_terms(grad_out, basis, activations, halves, n_row)
    marks = load(terms[1])
    received = [exchange(terms[mask], "row", n_row, mask) for mask in range(1, n_row)]
    inputs, _ = after(inputs, *received, *marks)
    far_inputs = [over_y(part, n_row) for part in inputs]
    core_input = exchange(whole, "row", n_row, 1)
    share = share_sum([terms[0]] + received, marks)
    if n_col == 8:
        marks = load(share)
        near = [share] + [exchange(share, "col", n_col, mask) for mask in (2, 4, 6)]
        near, ready = stack(near, marks)
        pieces = [near, exchange(near, "col", n_col, 1)]
    else:
        marks = load(share)
        pieces, ready = [lax.all_gather(share, "col", axis=1, tiled=True)], share
    ready = [pieces[-1], *load(ready)]

    moments, chunks = [], []
    for (at, _), cuts, part, far in zip(halves, parts_of, inputs, far_inputs):
        gathered = [[part], [core_input]] + with_core(far, ready, n_row, 2)
        new_first, new_second, direction, mark, *parts = adam_chunk(
            pieces, gathered, first_moment, second_moment, [], moments, at, cuts, n_row
        )
        moments, ready = [new_first, new_second], [mark]
        core = exchange(direction, "row", n_row, 1)
        for (start, width), part in zip(cuts, parts):
            chunks.append((at + start, start, [direction, core], over_y(part, n_row)))

    projector = pltpu.with_memory_space_constraint(projector, pltpu.VMEM)
    each = len(strips) // len(chunks)
    shape = weight.shape
    _, start, near, _ = chunks[0]
    *first_held, mark = weight_update(projector, shape, [], near=near, near_held=held[:each], start=start)
    held[:each] = first_held
    new_weight = []
    for index, (at, _, _, far) in enumerate(chunks):
        far = with_core(far, [mark], n_row, 2)
        here, there = slice(index * each, (index + 1) * each), slice((index + 1) * each, (index + 2) * each)
        _, start, near, _ = chunks[index + 1] if index + 1 < len(chunks) else (0, 0, (), 0)
        new, *moved, mark = weight_update(
            projector, shape, [], far, held[here], at, near, held[there], start, new_weight
        )
        new_weight = [new]
        held[there] = moved[each:]
    return (new_weight[0], *moments)


def solution(mesh):
    n_row, n_col = mesh.shape["row"], mesh.shape["col"]
    in_specs = (
        P("col", "row"),
        P("row", "col"),
        P("row", None),
        P("row", "col"),
        P("row", "col"),
        P("row", "col"),
    )
    out_specs = (P("row", "col"), P("row", "col"), P("row", "col"))
    return jax.shard_map(
        functools.partial(body, n_row, n_col),
        mesh=mesh,
        in_specs=in_specs,
        out_specs=out_specs,
        check_vma=False,
    )
```

time: 89.8 us -> 74.8 us (0.83)
  waiting for transfers between devices: 17.2 us -> 8.48 us
  Pallas kernels: 54.5 us -> 46.2 us
  starting transfers between devices: 16.9 us -> 18.9 us
    ppermute x23 -> x28, waiting for transfers between devices: 17.2 us -> 8.48 us  [exchange(): return lax.ppermute(values, axis, [(i, i ^ mask) for i in range(size)])]
    pallas_call x17, Pallas kernels: 50.2 us -> 41.7 us  [the longest x5 22.5 us: weight_update(): pl.pallas_call(functools.partial(update_kernel, far_at, start, height, co...]
    ppermute x23 -> x28, starting transfers between devices: 16.9 us -> 18.9 us  [exchange(): return lax.ppermute(values, axis, [(i, i ^ mask) for i in range(size)])]
  transfers between devices with their start and end apart: 23 -> 28, of which waited for: 8 -> 15; matrix products, arithmetic and copies ran while one was open for 0% -> 0% of each run, Pallas kernels for 48% -> 50%
where the time goes in v2:
time: 74.8 us; the launch traced here: 74.7 us
  Pallas kernels  46.2 us (62%)
  starting transfers between devices  18.9 us (25%)
  waiting for transfers between devices  8.48 us (11%)
  between operations  1.03 us (1%)
    pallas_call x5, Pallas kernels, weight_update(): pl.pallas_call(functools.partial(update_kernel, far_at, start, height, co...  22.5 us
    ppermute x28, starting transfers between devices, exchange(): return lax.ppermute(values, axis, [(i, i ^ mask) for i in range(size)])  18.9 us
    pallas_call x3, Pallas kernels, load_weight(): pl.pallas_call(functools.partial(load_kernel, cuts, height), out_shape=[p...  13.3 us
    ppermute x28, waiting for transfers between devices, exchange(): return lax.ppermute(values, axis, [(i, i ^ mask) for i in range(size)])  8.48 us
    pallas_call x2, Pallas kernels, adam_chunk(): pl.pallas_call(functools.partial(adam_kernel, counts, len(pieces), len(ma...  5.77 us
    pallas_call x1, Pallas kernels, lowered_terms(): pl.pallas_call(functools.partial(lowered_kernel, height, cuts), out_shape...  4.41 us
  transfers between devices with their start and end apart: 28, of which 15 were waited for; matrix products, arithmetic and copies ran while one was open for 0% of the time, Pallas kernels for 50%

profile of v2, /device:TPU:0, one launch (start us, length us, event | category | flops | bytes accessed | tf_op | source)
XLA Modules:
  0.0 74.7 jit_solution(533485841146299914)
XLA Ops:
  0.6 4.4 %lowered_terms.1 = (f32[128,256]{1,0:T(8,128)S(1)}, bf16[128,256]{1,0:T(8,128)(2,1)S(1)}, bf16[128,256]{1,0:T(8,128)(2,1)S(1)}, bf16[128,256]{1,0:T(8,128)(2,1)S...) custom-call(bf16[128,4096]{1,0:T(8,128)(2,1)} %grad_hbm.1, ...), custom_call_target="tpu_custom_call" | custom-call | flops 1 | bytes 1 | tf_op jit(solution)/shard_map/lowered_terms/pallas_call | solution.py:75
  5.6 2.6 %collective-permute-start.1 = (bf16[128,256]{1,0:T(8,128)(2,1)S(1)}, bf16[128,256]{1,0:T(8,128)(2,1)S(1)}, u32[]{:S(2)}, u32[]{:S(2)}) collective-permute-start(bf16[128,256]{1,0:T(8,128)(2,1)S(1)} %get-tuple-element.72), channel_id=1, source_target_pairs={{0,16},{8,24},{16,0},{24,8},{1,17},{9,25},{17,1},{25,9},{2,18},{10... | collective-permute-start | bytes 196616 | tf_op jit(solution)/shard_map/ppermute | solution.py:24
  8.4 3.5 %load_weight.3 = (f32[4096,256]{1,0:T(8,128)S(1)}, f32[4096,256]{1,0:T(8,128)S(1)}, bf16[16,128]{1,0:T(8,128)(2,1)S(1)}) custom-call(f32[4096,2048]{1,0:T(8,128)} %weight_hbm.5, bf16[128,256]{1,0:T(8,128)(2,1)S(1)} %get-tuple-element.71.mark_in), custom_call_target="tpu_custom_call" | custom-call | flops 1 | bytes 1 | tf_op jit(solution)/shard_map/load_weight/pallas_call | solution.py:113
  12.2 1.7 %collective-permute-start.9 = (bf16[256,1024]{1,0:T(8,128)(2,1)S(1)}, bf16[256,1024]{1,0:T(8,128)(2,1)S(1)}, u32[]{:S(2)}, u32[]{:S(2)}) collective-permute-start(bf16[256,1024]{1,0:T(8,128)(2,1)S(1)} %get-tuple-element.81.refs_2_), channel_id=1, source_target_pairs={{0,16},{8,24},{16,0},{24,8},{1,17},{9,25},{17,1},{25,9},{2,18},{10... | collective-permute-start | bytes 1572872 | tf_op jit(solution)/shard_map/ppermute | solution.py:24
  14.1 3.7 %collective-permute-start.5 = (bf16[256,128]{1,0:T(8,128)(2,1)S(1)}, bf16[256,128]{1,0:T(8,128)(2,1)S(1)}, u32[]{:S(2)}, u32[]{:S(2)}) collective-permute-start(bf16[256,128]{1,0:T(8,128)(2,1)S(1)} %share_sum.1.mark_in.refs_0_), channel_id=1, source_target_pairs={{0,6},{1,7},{2,4},{3,5},{4,2},{5,3},{6,0},{7,1},{8,14},{9,15},{10,... | collective-permute-start | bytes 196616 | tf_op jit(solution)/shard_map/ppermute | solution.py:24
  18.5 4.8 %load_weight.4 = (f32[4096,256]{1,0:T(8,128)S(1)}, f32[4096,256]{1,0:T(8,128)S(1)}, f32[4096,256]{1,0:T(8,128)S(1)}, bf16[16,128]{1,0:T(8,128)(2,1)S(1)}) custom-call(f32[4096,2048]{1,0:T(8,128)} %weight_hbm.5, bf16[256,128]{1,0:T(8,128)(2,1)S(1)} %share_sum.1.mark_in.refs_0_), custom_call_target="tpu_custom_call" | custom-call | flops 1 | bytes 1 | tf_op jit(solution)/shard_map/load_weight/pallas_call | solution.py:113
  23.4 1.6 %collective-permute-start.6 = (bf16[1024,128]{1,0:T(8,128)(2,1)S(1)}, bf16[1024,128]{1,0:T(8,128)(2,1)S(1)}, u32[]{:S(2)}, u32[]{:S(2)}) collective-permute-start(bf16[1024,128]{1,0:T(8,128)(2,1)S(1)} %get-tuple-element.76.refs_0_), channel_id=1, source_target_pairs={{0,1},{1,0},{2,3},{3,2},{4,5},{5,4},{6,7},{7,6},{8,9},{9,8},{10,11... | collective-permute-start | bytes 786440 | tf_op jit(solution)/shard_map/ppermute | solution.py:24
  25.5 4.9 %load_weight.5 = (f32[4096,256]{1,0:T(8,128)S(1)}, f32[4096,256]{1,0:T(8,128)S(1)}, f32[4096,256]{1,0:T(8,128)S(1)}, bf16[16,128]{1,0:T(8,128)(2,1)S(1)}) custom-call(f32[4096,2048]{1,0:T(8,128)} %weight_hbm.5, bf16[16,128]{1,0:T(8,128)(2,1)S(1)} %get-tuple-element.82.mark_in), custom_call_target="tpu_custom_call" | custom-call | flops 1 | bytes 1 | tf_op jit(solution)/shard_map/load_weight/pallas_call | solution.py:113
  30.4 1.1 %collective-permute-done.6.refs_1_ = bf16[1024,128]{1,0:T(8,128)(2,1)S(1)} collective-permute-done((bf16[1024,128]{1,0:T(8,128)(2,1)S(1)}, bf16[1024,128]{1,0:T(8,128)(2,1)S(1)}, u32[]{:S(2)}, u32[]{:S(2)}) %collective-permute-start.6) | collective-permute-done | bytes 262176 | tf_op jit(solution)/shard_map/ppermute | solution.py:24
  32.1 1.0 %collective-permute-done.10.refs_5_ = bf16[256,512]{1,0:T(8,128)(2,1)S(1)} collective-permute-done((bf16[256,512]{1,0:T(8,128)(2,1)S(1)}, bf16[256,512]{1,0:T(8,128)(2,1)S(1)}, u32[]{:S(2)}, u32[]{:S(2)}) %collective-permute-start.10) | collective-permute-done | bytes 262176 | tf_op jit(solution)/shard_map/ppermute | solution.py:24
  33.6 2.6 %adam_chunk.2 = (f32[256,2048]{1,0:T(8,128)}, f32[256,2048]{1,0:T(8,128)}, bf16[256,1024]{1,0:T(8,128)(2,1)S(1)}, bf16[16,128]{1,0:T(8,128)(2,1)S(1)}, bf16[256,...) custom-call(bf16[1024,128]{1,0:T(8,128)(2,1)S(1)} %get-tuple-element.76.refs_0_, ...), custom_call_target="tpu_custom_call" | custom-call | flops 1 | bytes 1 | tf_op jit(solution)/shard_map/adam_chunk/pallas_call | solution.py:224
  36.4 2.0 %collective-permute-done.8.refs_0_ = bf16[256,1024]{1,0:T(8,128)(2,1)S(1)} collective-permute-done((bf16[256,1024]{1,0:T(8,128)(2,1)S(1)}, bf16[256,1024]{1,0:T(8,128)(2,1)S(1)}, u32[]{:S(2)}, u32[]{:S(2)}) %collective-permute-start.8) | collective-permute-done | bytes 524320 | tf_op jit(solution)/shard_map/ppermute | solution.py:24
  39.0 0.8 %collective-permute-start.17 = (bf16[256,512]{1,0:T(8,128)(2,1)S(1)}, bf16[256,512]{1,0:T(8,128)(2,1)S(1)}, u32[]{:S(2)}, u32[]{:S(2)}) collective-permute-start(bf16[256,512]{1,0:T(8,128)(2,1)S(1)} %get-tuple-element.96), channel_id=1, source_target_pairs={{0,16},{8,24},{16,0},{24,8},{1,17},{9,25},{17,1},{25,9},{2,18},{10... | collective-permute-start | bytes 786440 | tf_op jit(solution)/shard_map/ppermute | solution.py:24
  40.4 3.2 %adam_chunk.3 = (f32[256,2048]{1,0:T(8,128)}, f32[256,2048]{1,0:T(8,128)}, bf16[256,1024]{1,0:T(8,128)(2,1)S(1)}, bf16[16,128]{1,0:T(8,128)(2,1)}, bf16[256,512]...) custom-call(bf16[1024,128]{1,0:T(8,128)(2,1)S(1)} %get-tuple-element.76.refs_0_, ...), custom_call_target="tpu_custom_call", output_to_operand_aliasing={{0}: (9, {}), {1}: (10, {})} | custom-call | flops 1 | bytes 1 | tf_op jit(solution)/shard_map/adam_chunk/pallas_call | solution.py:224
  43.8 0.8 %collective-permute-start.16 = (bf16[256,512]{1,0:T(8,128)(2,1)S(1)}, bf16[256,512]{1,0:T(8,128)(2,1)S(1)}, u32[]{:S(2)}, u32[]{:S(2)}) collective-permute-start(bf16[256,512]{1,0:T(8,128)(2,1)S(1)} %get-tuple-element.95), channel_id=1, source_target_pairs={{0,16},{8,24},{16,0},{24,8},{1,17},{9,25},{17,1},{25,9},{2,18},{10... | collective-permute-start | bytes 786440 | tf_op jit(solution)/shard_map/ppermute | solution.py:24
  44.6 2.5 %weight_update.5 = (f32[4096,256]{1,0:T(8,128)S(1)}, f32[4096,256]{1,0:T(8,128)S(1)}, bf16[16,128]{1,0:T(8,128)(2,1)S(1)}) custom-call(bf16[4096,1024]{1,0:T(8,128)(2,1)S(1)} %bitcast.1, bf16[256,1024]{1,0:T(8,128)(2,1)S(1)} %get-tuple-element.97.refs_0_.refs_3_, ...), custom_call_target="tpu_custom_call", output_to_operand_aliasing={{0}: (3, {}), {1}: (4, {})} | custom-call | flops 1 | bytes 1 | tf_op jit(solution)/shard_map/weight_update/pallas_call | solution.py:314
  48.3 0.8 %collective-permute-start.15 = (bf16[256,512]{1,0:T(8,128)(2,1)S(1)}, bf16[256,512]{1,0:T(8,128)(2,1)S(1)}, u32[]{:S(2)}, u32[]{:S(2)}) collective-permute-start(bf16[256,512]{1,0:T(8,128)(2,1)S(1)} %get-tuple-element.94), channel_id=1, source_target_pairs={{0,16},{8,24},{16,0},{24,8},{1,17},{9,25},{17,1},{25,9},{2,18},{10... | collective-permute-start | bytes 786440 | tf_op jit(solution)/shard_map/ppermute | solution.py:24
  49.3 5.0 %weight_update.6 = (f32[4096,2048]{1,0:T(8,128)}, f32[4096,256]{1,0:T(8,128)S(1)}, f32[4096,256]{1,0:T(8,128)S(1)}, f32[4096,256]{1,0:T(8,128)S(1)}, f32[4096,25...) custom-call(bf16[4096,1024]{1,0:T(8,128)(2,1)S(1)} %bitcast.1, ...), custom_call_target="tpu_custom_call", output_to_operand_aliasing={{1}: (6, {}), {2}: (7, {}), {3}: (8, {}), {4}: (9, {})} | custom-call | flops 1 | bytes 1 | tf_op jit(solution)/shard_map/weight_update/pallas_call | solution.py:314
  55.0 1.0 %collective-permute-start.14 = (bf16[256,512]{1,0:T(8,128)(2,1)S(1)}, bf16[256,512]{1,0:T(8,128)(2,1)S(1)}, u32[]{:S(2)}, u32[]{:S(2)}) collective-permute-start(bf16[256,512]{1,0:T(8,128)(2,1)S(1)} %get-tuple-element.93), channel_id=1, source_target_pairs={{0,16},{8,24},{16,0},{24,8},{1,17},{9,25},{17,1},{25,9},{2,18},{10... | collective-permute-start | bytes 786440 | tf_op jit(solution)/shard_map/ppermute | solution.py:24
  56.1 5.3 %weight_update.7 = (f32[4096,2048]{1,0:T(8,128)}, f32[4096,256]{1,0:T(8,128)S(1)}, f32[4096,256]{1,0:T(8,128)S(1)}, f32[4096,256]{1,0:T(8,128)S(1)}, f32[4096,25...) custom-call(bf16[4096,1024]{1,0:T(8,128)(2,1)S(1)} %bitcast.1, ...), custom_call_target="tpu_custom_call", output_to_operand_aliasing={{1}: (6, {}), {2}: (7, {}), {3}: (8, {}), {4}: (9, {}), {0}... | custom-call | flops 1 | bytes 1 | tf_op jit(solution)/shard_map/weight_update/pallas_call | solution.py:314
  62.1 0.8 %collective-permute-done.24.refs_1_ = bf16[256,256]{1,0:T(8,128)(2,1)S(1)} collective-permute-done((bf16[256,256]{1,0:T(8,128)(2,1)S(1)}, bf16[256,256]{1,0:T(8,128)(2,1)S(1)}, u32[]{:S(2)}, u32[]{:S(2)}) %collective-permute-start.24) | collective-permute-done | bytes 131104 | tf_op jit(solution)/shard_map/ppermute | solution.py:24
  63.1 5.1 %weight_update.8 = (f32[4096,2048]{1,0:T(8,128)}, f32[4096,256]{1,0:T(8,128)S(1)}, f32[4096,256]{1,0:T(8,128)S(1)}, f32[4096,256]{1,0:T(8,128)S(1)}, f32[4096,25...) custom-call(bf16[4096,1024]{1,0:T(8,128)(2,1)S(1)} %bitcast.1, ...), custom_call_target="tpu_custom_call", output_to_operand_aliasing={{1}: (6, {}), {2}: (7, {}), {3}: (8, {}), {4}: (9, {}), {0}... | custom-call | flops 1 | bytes 1 | tf_op jit(solution)/shard_map/weight_update/pallas_call | solution.py:314
  68.8 0.8 %collective-permute-done.26.refs_1_ = bf16[256,256]{1,0:T(8,128)(2,1)S(1)} collective-permute-done((bf16[256,256]{1,0:T(8,128)(2,1)S(1)}, bf16[256,256]{1,0:T(8,128)(2,1)S(1)}, u32[]{:S(2)}, u32[]{:S(2)}) %collective-permute-start.26) | collective-permute-done | bytes 131104 | tf_op jit(solution)/shard_map/ppermute | solution.py:24
  70.0 4.5 %weight_update.9 = (f32[4096,2048]{1,0:T(8,128)}, f32[4096,256]{1,0:T(8,128)S(1)}, f32[4096,256]{1,0:T(8,128)S(1)}, bf16[16,128]{1,0:T(8,128)(2,1)}) custom-call(bf16[4096,1024]{1,0:T(8,128)(2,1)S(1)} %bitcast.1, bf16[256,512]{1,0:T(8,128)(2,1)S(1)} %get-tuple-element.128.refs_0_, ...), custom_call_target="tpu_custom_call", output_to_operand_aliasing={{1}: (4, {}), {2}: (5, {}), {0}: (6, {})} | custom-call | flops 1 | bytes 1 | tf_op jit(solution)/shard_map/weight_update/pallas_call | solution.py:314
  (61 shorter events, 8.9 us)
Async XLA Ops:
  5.0 28.5 %collective-permute-start.7 = (bf16[256,2048]{1,0:T(8,128)(2,1)S(1)}, bf16[256,2048]{1,0:T(8,128)(2,1)S(1)}, u32[]{:S(2)}, u32[]{:S(2)}) collective-permute-start(bf16[256,2048]{1,0:T(8,128)(2,1)S(1)} %get-tuple-element.80), channel_id=1, source_target_pairs={{0,8},{8,0},{16,24},{24,16},{1,9},{9,1},{17,25},{25,17},{2,10},{10... | collective-permute-start | bytes 3145736 | tf_op jit(solution)/shard_map/ppermute | solution.py:24
  5.6 6.3 %collective-permute-start.1 = (bf16[128,256]{1,0:T(8,128)(2,1)S(1)}, bf16[128,256]{1,0:T(8,128)(2,1)S(1)}, u32[]{:S(2)}, u32[]{:S(2)}) collective-permute-start(bf16[128,256]{1,0:T(8,128)(2,1)S(1)} %get-tuple-element.72), channel_id=1, source_target_pairs={{0,16},{8,24},{16,0},{24,8},{1,17},{9,25},{17,1},{25,9},{2,18},{10... | collective-permute-start | bytes 196616 | tf_op jit(solution)/shard_map/ppermute | solution.py:24
  8.2 4.0 %collective-permute-start.2 = (bf16[128,256]{1,0:T(8,128)(2,1)S(1)}, bf16[128,256]{1,0:T(8,128)(2,1)S(1)}, u32[]{:S(2)}, u32[]{:S(2)}) collective-permute-start(bf16[128,256]{1,0:T(8,128)(2,1)S(1)} %get-tuple-element.73), channel_id=1, source_target_pairs={{0,24},{8,16},{16,8},{24,0},{1,25},{9,17},{17,9},{25,1},{2,26},{10... | collective-permute-start | bytes 196616 | tf_op jit(solution)/shard_map/ppermute | solution.py:24
  8.2 4.0 %collective-permute-start = (bf16[128,256]{1,0:T(8,128)(2,1)S(1)}, bf16[128,256]{1,0:T(8,128)(2,1)S(1)}, u32[]{:S(2)}, u32[]{:S(2)}) collective-permute-start(bf16[128,256]{1,0:T(8,128)(2,1)S(1)} %get-tuple-element.71.mark_in), channel_id=1, source_target_pairs={{0,8},{8,0},{16,24},{24,16},{1,9},{9,1},{17,25},{25,17},{2,10},{10... | collective-permute-start | bytes 196616 | tf_op jit(solution)/shard_map/ppermute | solution.py:24
  12.2 19.3 %collective-permute-start.9 = (bf16[256,1024]{1,0:T(8,128)(2,1)S(1)}, bf16[256,1024]{1,0:T(8,128)(2,1)S(1)}, u32[]{:S(2)}, u32[]{:S(2)}) collective-permute-start(bf16[256,1024]{1,0:T(8,128)(2,1)S(1)} %get-tuple-element.81.refs_2_), channel_id=1, source_target_pairs={{0,16},{8,24},{16,0},{24,8},{1,17},{9,25},{17,1},{25,9},{2,18},{10... | collective-permute-start | bytes 1572872 | tf_op jit(solution)/shard_map/ppermute | solution.py:24
  14.1 9.3 %collective-permute-start.5 = (bf16[256,128]{1,0:T(8,128)(2,1)S(1)}, bf16[256,128]{1,0:T(8,128)(2,1)S(1)}, u32[]{:S(2)}, u32[]{:S(2)}) collective-permute-start(bf16[256,128]{1,0:T(8,128)(2,1)S(1)} %share_sum.1.mark_in.refs_0_), channel_id=1, source_target_pairs={{0,6},{1,7},{2,4},{3,5},{4,2},{5,3},{6,0},{7,1},{8,14},{9,15},{10,... | collective-permute-start | bytes 196616 | tf_op jit(solution)/shard_map/ppermute | solution.py:24
  17.7 5.7 %collective-permute-start.4 = (bf16[256,128]{1,0:T(8,128)(2,1)S(1)}, bf16[256,128]{1,0:T(8,128)(2,1)S(1)}, u32[]{:S(2)}, u32[]{:S(2)}) collective-permute-start(bf16[256,128]{1,0:T(8,128)(2,1)S(1)} %share_sum.1.mark_in.refs_0_), channel_id=1, source_target_pairs={{0,4},{1,5},{2,6},{3,7},{4,0},{5,1},{6,2},{7,3},{8,12},{9,13},{10,... | collective-permute-start | bytes 196616 | tf_op jit(solution)/shard_map/ppermute | solution.py:24
  17.7 5.7 %collective-permute-start.3 = (bf16[256,128]{1,0:T(8,128)(2,1)S(1)}, bf16[256,128]{1,0:T(8,128)(2,1)S(1)}, u32[]{:S(2)}, u32[]{:S(2)}) collective-permute-start(bf16[256,128]{1,0:T(8,128)(2,1)S(1)} %share_sum.1.mark_in.refs_0_), channel_id=1, source_target_pairs={{0,2},{1,3},{2,0},{3,1},{4,6},{5,7},{6,4},{7,5},{8,10},{9,11},{10,... | collective-permute-start | bytes 196616 | tf_op jit(solution)/shard_map/ppermute | solution.py:24
  23.4 8.1 %collective-permute-start.6 = (bf16[1024,128]{1,0:T(8,128)(2,1)S(1)}, bf16[1024,128]{1,0:T(8,128)(2,1)S(1)}, u32[]{:S(2)}, u32[]{:S(2)}) collective-permute-start(bf16[1024,128]{1,0:T(8,128)(2,1)S(1)} %get-tuple-element.76.refs_0_), channel_id=1, source_target_pairs={{0,1},{1,0},{2,3},{3,2},{4,5},{5,4},{6,7},{7,6},{8,9},{9,8},{10,11... | collective-permute-start | bytes 786440 | tf_op jit(solution)/shard_map/ppermute | solution.py:24
  25.0 13.4 %collective-permute-start.8 = (bf16[256,1024]{1,0:T(8,128)(2,1)S(1)}, bf16[256,1024]{1,0:T(8,128)(2,1)S(1)}, u32[]{:S(2)}, u32[]{:S(2)}) collective-permute-start(bf16[256,1024]{1,0:T(8,128)(2,1)S(1)} %get-tuple-element.79.refs_2_), channel_id=1, source_target_pairs={{0,16},{8,24},{16,0},{24,8},{1,17},{9,25},{17,1},{25,9},{2,18},{10... | collective-permute-start | bytes 1572872 | tf_op jit(solution)/shard_map/ppermute | solution.py:24
  31.6 1.6 %collective-permute-start.10 = (bf16[256,512]{1,0:T(8,128)(2,1)S(1)}, bf16[256,512]{1,0:T(8,128)(2,1)S(1)}, u32[]{:S(2)}, u32[]{:S(2)}) collective-permute-start(bf16[256,512]{1,0:T(8,128)(2,1)S(1)} %get-tuple-element.85), channel_id=1, source_target_pairs={{0,8},{8,0},{16,24},{24,16},{1,9},{9,1},{17,25},{25,17},{2,10},{10... | collective-permute-start | bytes 786440 | tf_op jit(solution)/shard_map/ppermute | solution.py:24
  31.6 1.9 %collective-permute-start.11 = (bf16[256,512]{1,0:T(8,128)(2,1)S(1)}, bf16[256,512]{1,0:T(8,128)(2,1)S(1)}, u32[]{:S(2)}, u32[]{:S(2)}) collective-permute-start(bf16[256,512]{1,0:T(8,128)(2,1)S(1)} %get-tuple-element.86), channel_id=1, source_target_pairs={{0,8},{8,0},{16,24},{24,16},{1,9},{9,1},{17,25},{25,17},{2,10},{10... | collective-permute-start | bytes 786440 | tf_op jit(solution)/shard_map/ppermute | solution.py:24
  36.2 8.4 %collective-permute-start.18 = (bf16[256,1024]{1,0:T(8,128)(2,1)S(1)}, bf16[256,1024]{1,0:T(8,128)(2,1)S(1)}, u32[]{:S(2)}, u32[]{:S(2)}) collective-permute-start(bf16[256,1024]{1,0:T(8,128)(2,1)S(1)} %get-tuple-element.97.refs_0_.refs_3_), channel_id=1, source_target_pairs={{0,8},{8,0},{16,24},{24,16},{1,9},{9,1},{17,25},{25,17},{2,10},{10... | collective-permute-start | bytes 1572872 | tf_op jit(solution)/shard_map/ppermute | solution.py:24
  38.4 1.6 %collective-permute-start.12 = (bf16[256,512]{1,0:T(8,128)(2,1)S(1)}, bf16[256,512]{1,0:T(8,128)(2,1)S(1)}, u32[]{:S(2)}, u32[]{:S(2)}) collective-permute-start(bf16[256,512]{1,0:T(8,128)(2,1)S(1)} %get-tuple-element.89), channel_id=1, source_target_pairs={{0,8},{8,0},{16,24},{24,16},{1,9},{9,1},{17,25},{25,17},{2,10},{10... | collective-permute-start | bytes 786440 | tf_op jit(solution)/shard_map/ppermute | solution.py:24
  38.5 1.9 %collective-permute-start.13 = (bf16[256,512]{1,0:T(8,128)(2,1)S(1)}, bf16[256,512]{1,0:T(8,128)(2,1)S(1)}, u32[]{:S(2)}, u32[]{:S(2)}) collective-permute-start(bf16[256,512]{1,0:T(8,128)(2,1)S(1)} %get-tuple-element.90), channel_id=1, source_target_pairs={{0,8},{8,0},{16,24},{24,16},{1,9},{9,1},{17,25},{25,17},{2,10},{10... | collective-permute-start | bytes 786440 | tf_op jit(solution)/shard_map/ppermute | solution.py:24
  39.0 8.8 %collective-permute-start.17 = (bf16[256,512]{1,0:T(8,128)(2,1)S(1)}, bf16[256,512]{1,0:T(8,128)(2,1)S(1)}, u32[]{:S(2)}, u32[]{:S(2)}) collective-permute-start(bf16[256,512]{1,0:T(8,128)(2,1)S(1)} %get-tuple-element.96), channel_id=1, source_target_pairs={{0,16},{8,24},{16,0},{24,8},{1,17},{9,25},{17,1},{25,9},{2,18},{10... | collective-permute-start | bytes 786440 | tf_op jit(solution)/shard_map/ppermute | solution.py:24
  43.6 12.5 %collective-permute-start.23 = (bf16[256,1024]{1,0:T(8,128)(2,1)S(1)}, bf16[256,1024]{1,0:T(8,128)(2,1)S(1)}, u32[]{:S(2)}, u32[]{:S(2)}) collective-permute-start(bf16[256,1024]{1,0:T(8,128)(2,1)S(1)} %get-tuple-element.112.refs_3_), channel_id=1, source_target_pairs={{0,8},{8,0},{16,24},{24,16},{1,9},{9,1},{17,25},{25,17},{2,10},{10... | collective-permute-start | bytes 1572872 | tf_op jit(solution)/shard_map/ppermute | solution.py:24
  43.8 10.6 %collective-permute-start.16 = (bf16[256,512]{1,0:T(8,128)(2,1)S(1)}, bf16[256,512]{1,0:T(8,128)(2,1)S(1)}, u32[]{:S(2)}, u32[]{:S(2)}) collective-permute-start(bf16[256,512]{1,0:T(8,128)(2,1)S(1)} %get-tuple-element.95), channel_id=1, source_target_pairs={{0,16},{8,24},{16,0},{24,8},{1,17},{9,25},{17,1},{25,9},{2,18},{10... | collective-permute-start | bytes 786440 | tf_op jit(solution)/shard_map/ppermute | solution.py:24
  47.7 1.4 %collective-permute-start.19 = (bf16[256,256]{1,0:T(8,128)(2,1)S(1)}, bf16[256,256]{1,0:T(8,128)(2,1)S(1)}, u32[]{:S(2)}, u32[]{:S(2)}) collective-permute-start(bf16[256,256]{1,0:T(8,128)(2,1)S(1)} %get-tuple-element.102), channel_id=1, source_target_pairs={{0,8},{8,0},{16,24},{24,16},{1,9},{9,1},{17,25},{25,17},{2,10},{10... | collective-permute-start | bytes 393224 | tf_op jit(solution)/shard_map/ppermute | solution.py:24
  47.8 1.5 %collective-permute-start.20 = (bf16[256,256]{1,0:T(8,128)(2,1)S(1)}, bf16[256,256]{1,0:T(8,128)(2,1)S(1)}, u32[]{:S(2)}, u32[]{:S(2)}) collective-permute-start(bf16[256,256]{1,0:T(8,128)(2,1)S(1)} %get-tuple-element.103), channel_id=1, source_target_pairs={{0,8},{8,0},{16,24},{24,16},{1,9},{9,1},{17,25},{25,17},{2,10},{10... | collective-permute-start | bytes 393224 | tf_op jit(solution)/shard_map/ppermute | solution.py:24
  48.3 13.1 %collective-permute-start.15 = (bf16[256,512]{1,0:T(8,128)(2,1)S(1)}, bf16[256,512]{1,0:T(8,128)(2,1)S(1)}, u32[]{:S(2)}, u32[]{:S(2)}) collective-permute-start(bf16[256,512]{1,0:T(8,128)(2,1)S(1)} %get-tuple-element.94), channel_id=1, source_target_pairs={{0,16},{8,24},{16,0},{24,8},{1,17},{9,25},{17,1},{25,9},{2,18},{10... | collective-permute-start | bytes 786440 | tf_op jit(solution)/shard_map/ppermute | solution.py:24
  54.4 1.6 %collective-permute-start.21 = (bf16[256,256]{1,0:T(8,128)(2,1)S(1)}, bf16[256,256]{1,0:T(8,128)(2,1)S(1)}, u32[]{:S(2)}, u32[]{:S(2)}) collective-permute-start(bf16[256,256]{1,0:T(8,128)(2,1)S(1)} %get-tuple-element.110), channel_id=1, source_target_pairs={{0,8},{8,0},{16,24},{24,16},{1,9},{9,1},{17,25},{25,17},{2,10},{10... | collective-permute-start | bytes 393224 | tf_op jit(solution)/shard_map/ppermute | solution.py:24
  55.0 13.2 %collective-permute-start.14 = (bf16[256,512]{1,0:T(8,128)(2,1)S(1)}, bf16[256,512]{1,0:T(8,128)(2,1)S(1)}, u32[]{:S(2)}, u32[]{:S(2)}) collective-permute-start(bf16[256,512]{1,0:T(8,128)(2,1)S(1)} %get-tuple-element.93), channel_id=1, source_target_pairs={{0,16},{8,24},{16,0},{24,8},{1,17},{9,25},{17,1},{25,9},{2,18},{10... | collective-permute-start | bytes 786440 | tf_op jit(solution)/shard_map/ppermute | solution.py:24
  61.5 1.4 %collective-permute-start.24 = (bf16[256,256]{1,0:T(8,128)(2,1)S(1)}, bf16[256,256]{1,0:T(8,128)(2,1)S(1)}, u32[]{:S(2)}, u32[]{:S(2)}) collective-permute-start(bf16[256,256]{1,0:T(8,128)(2,1)S(1)} %get-tuple-element.120), channel_id=1, source_target_pairs={{0,8},{8,0},{16,24},{24,16},{1,9},{9,1},{17,25},{25,17},{2,10},{10... | collective-permute-start | bytes 393224 | tf_op jit(solution)/shard_map/ppermute | solution.py:24
  (8 other events, 36.9 us)

commit v3 on v2

--- a/solution.py
+++ b/solution.py
@@ -170,8 +170,8 @@
         inputs.append(refs[:count])
         refs = refs[count:]
     first_ref, second_ref, refs = refs[0], refs[1], refs[2 + n_skip :]
-    new_first_ref, new_second_ref, direction_ref, mark_ref = refs[:4]
-    part_refs, (lowered_ref, firsts, seconds, sems) = refs[4:-4], refs[-4:]
+    new_first_ref, new_second_ref, mark_ref = refs[:3]
+    part_refs, (lowered_ref, firsts, seconds, sems) = refs[3:-4], refs[-4:]
     mark_ref[...] = jnp.zeros_like(mark_ref)
     depth, width = inputs[0][0].shape
     row, col = lax.axis_index("row"), lax.axis_index("col")
@@ -185,7 +185,6 @@
         lowered_ref[...] = pieces[0][...]
     copies = []
     for number, at in enumerate(range(0, width, step)):
-        here = slice(at, at + step)
         there = slice(offset + at, offset + at + step)
         lowgrad = None
         for mask, blocks in enumerate(inputs):
@@ -206,9 +205,10 @@
         corrected_first = new_first / (1.0 - first_decay**STEP)
         corrected_second = new_second / (1.0 - second_decay**STEP)
         direction = corrected_first / (jnp.sqrt(corrected_second) + adam_epsilon)
-        direction_ref[:, here] = (learn_rate * direction).astype(direction_ref.dtype)
-    for (at, width), part_ref in zip(cuts, part_refs):
-        part_ref[...] = direction_ref[:, at : at + width]
+        for (begin, part_width), part_ref in zip(cuts, part_refs):
+            if begin <= at < begin + part_width:
+                here = slice(at - begin, at - begin + step)
+                part_ref[:, here] = (learn_rate * direction).astype(part_ref.dtype)
     for copy in copies:
         copy.wait()
 
@@ -226,12 +226,11 @@
         out_shape=[
             jax.ShapeDtypeStruct(first.shape, jnp.float32),
             jax.ShapeDtypeStruct(first.shape, jnp.float32),
-            jax.ShapeDtypeStruct((ranks, width), jnp.bfloat16),
             MARK,
             *(jax.ShapeDtypeStruct((ranks, part), jnp.bfloat16) for _, part in cuts),
         ],
         in_specs=[VMEM] * n_plain + [ANY] * len(carried),
-        out_specs=[ANY, ANY, VMEM, VMEM] + [VMEM] * len(cuts),
+        out_specs=[ANY, ANY] + [VMEM] * (1 + len(cuts)),
         scratch_shapes=[
             pltpu.VMEM((ranks, tokens), jnp.bfloat16),
             pltpu.VMEM((count, ranks, step), jnp.float32),
@@ -245,25 +244,24 @@
     )(*pieces, *sum(inputs, []), first, second, *marks, *carried)
 
 
-def gather_pair(pair, parts, start):
+def gather_pair(pair, parts):
     core = lax.rem(lax.axis_index("row"), 2)
-    width = pair.shape[1]
     ranks = parts[0][0].shape[0]
     for mask, pieces in enumerate(parts):
         rows = pl.ds(pl.multiple_of((core ^ mask) * ranks, ranks), ranks)
-        span = min(width, pieces[0].shape[1])
+        span = pieces[0].shape[1]
         for index, piece in enumerate(pieces):
-            pair[rows, index * span : (index + 1) * span] = piece[:, start : start + span]
-
-
-def update_kernel(far_at, start, height, far_counts, n_near, n_far_held, n_near_held, n_skip, basis_ref, *refs):
+            pair[rows, index * span : (index + 1) * span] = piece[...]
+
+
+def update_kernel(far_at, height, near_steps, masks, final, counts, n_near, n_far_held, n_near_held, n_skip, basis_ref, *refs):
     far_parts = []
-    for count in far_counts:
+    for count in counts:
         far_parts.append(refs[:count])
         refs = refs[count:]
-    near_parts = [[part] for part in refs[:n_near]]
+    near_parts, far_parts = far_parts[:n_near], far_parts[n_near:]
     n_held = n_far_held + n_near_held
-    refs = refs[n_near + n_held + n_skip :]
+    refs = refs[n_held + n_skip :]
     outs, held_refs = refs[: len(refs) - n_held - 3], refs[-n_held - 3 : -3]
     mark_ref, pairs, sems = refs[-3:]
     span = held_refs[0].shape[1]
@@ -271,55 +269,67 @@
     ranks = pairs.shape[1] // 2
     chip = lax.axis_index("row") // 2
 
-    def subtract(rows, helds, mask, pair):
-        taken = pl.ds(pl.multiple_of((chip ^ mask) * 2 * ranks, 2 * ranks), 2 * ranks)
+    def subtract(rows, helds, first, depth, pair):
+        taken = pl.ds(pl.multiple_of(first * depth, depth), depth)
         update = jnp.dot(basis_ref[rows, taken], pair, preferred_element_type=jnp.float32)
         for index, held in enumerate(helds):
             held[rows, :] = held[rows, :] - update[:, index * span : (index + 1) * span]
 
     copies = []
-    for index in range(0, len(far_parts), 2):
-        gather_pair(pairs.at[index // 2 + 1], far_parts[index : index + 2], 0)
+    row = lax.axis_index("row")
+    terms = []
+    for index in range(0, len(far_parts), 1 if masks else 2):
+        if masks:
+            span_in = far_parts[index][0].shape[1]
+            for number, piece in enumerate(far_parts[index]):
+                pairs[index + 1, :ranks, number * span_in : (number + 1) * span_in] = piece[...]
+            terms.append((row ^ masks[index], ranks, pairs.at[index + 1, :ranks]))
+        else:
+            gather_pair(pairs.at[index // 2 + 1], far_parts[index : index + 2])
+            terms.append((chip ^ (index // 2 + 1), 2 * ranks, pairs.at[index // 2 + 1]))
     if n_near:
-        gather_pair(pairs.at[0], near_parts, start)
+        gather_pair(pairs.at[0], near_parts)
     for step in range(count if far_parts else 0):
         rows = slice(step * height, (step + 1) * height)
-        for index in range(0, len(far_parts), 2):
-            subtract(rows, held_refs[:n_far_held], index // 2 + 1, pairs[index // 2 + 1])
-        for index, held in enumerate(held_refs[:n_far_held]):
+        for first, depth, pair in terms:
+            subtract(rows, held_refs[:n_far_held], first, depth, pair[...])
+        for index, held in enumerate(held_refs[:n_far_held] if final else ()):
             target = outs[0].at[rows, far_at + index * span : far_at + (index + 1) * span]
             copies.append(pltpu.make_async_copy(held.at[rows], target, sems.at[step, index]))
             copies[-1].start()
-    for step in range(count if n_near else 0):
+    for step in near_steps:
         rows = slice(step * height, (step + 1) * height)
-        subtract(rows, held_refs[n_far_held:], 0, pairs[0])
+        subtract(rows, held_refs[n_far_held:], chip, 2 * ranks, pairs[0])
     mark_ref[...] = jnp.zeros_like(mark_ref)
     for copy in copies:
         copy.wait()
 
 
-def weight_update(projector, shape, marks, far=(), far_held=(), far_at=0, near=(), near_held=(), start=0, carried=()):
+def weight_update(projector, shape, marks, far=(), far_held=(), far_at=0, near=(), near_held=(), part=(0, 1), masks=(), final=True, carried=()):
     helds = [*far_held, *near_held]
-    counts = [len(pieces) for pieces in far]
-    flat = sum(far, []) + list(near)
+    counts = [len(pieces) for pieces in [*near, *far]]
+    flat = sum([*near, *far], [])
     rows, span = helds[0].shape
     ranks, width = flat[0].shape[0], span * max(len(far_held), len(near_held))
     height = min(512, rows)
+    begin, end = (int(edge * (rows // height)) for edge in part)
+    near_steps = range(begin, end) if near else ()
     n_plain = 1 + len(flat)
-    out_shape = [jax.ShapeDtypeStruct(shape, jnp.float32)] if far else []
+    final = final and bool(far)
+    out_shape = [jax.ShapeDtypeStruct(shape, jnp.float32)] if final else []
     aliases = {n_plain + index: len(out_shape) + index for index in range(len(helds))}
     if carried:
         aliases[n_plain + len(helds) + len(marks)] = 0
     n_skip = len(marks) + len(carried)
     return pl.pallas_call(
         functools.partial(
-            update_kernel, far_at, start, height, counts, len(near), len(far_held), len(near_held), n_skip
+            update_kernel, far_at, height, near_steps, masks, final, counts, len(near), len(far_held), len(near_held), n_skip
         ),
         out_shape=out_shape + [pltpu.VMEM(held.shape, jnp.float32) for held in helds] + [MARK],
         in_specs=[VMEM] * (n_plain + len(helds) + len(marks)) + [ANY] * len(carried),
         out_specs=[ANY] * len(out_shape) + [VMEM] * (len(helds) + 1),
         scratch_shapes=[
-            pltpu.VMEM((1 + len(far) // 2, 2 * ranks, width), jnp.bfloat16),
+            pltpu.VMEM((1 + (len(far) if masks else len(far) // 2), 2 * ranks, width), jnp.bfloat16),
             pltpu.SemaphoreType.DMA((rows // height, max(1, len(far_held)))),
         ],
         input_output_aliases=aliases,
@@ -382,7 +392,7 @@
     ]
     total = activations.shape[1]
     halves = cut(total, (1, 1))
-    parts_of = [cut(width, (1, 1)) for _, width in halves]
+    parts_of = [[(0, halves[0][1])] + cut(halves[0][1], (1,) * pieces) for pieces in (2, 4)]
     strips = cut(total, (1,) * 8)
     loads = [strips[6:], strips[3:6], strips[:3]]
     held = []
@@ -413,33 +423,48 @@
         pieces, ready = [lax.all_gather(share, "col", axis=1, tiled=True)], share
     ready = [pieces[-1], *load(ready)]
 
-    moments, chunks = [], []
+    projector = pltpu.with_memory_space_constraint(projector, pltpu.VMEM)
+    each, shape = len(strips) // len(halves), weight.shape
+    moments, chunks, marks = [], [], []
     for (at, _), cuts, part, far in zip(halves, parts_of, inputs, far_inputs):
-        gathered = [[part], [core_input]] + with_core(far, ready, n_row, 2)
-        new_first, new_second, direction, mark, *parts = adam_chunk(
-            pieces, gathered, first_moment, second_moment, [], moments, at, cuts, n_row
+        gathered = [[part], [core_input]] + with_core(far, ready, n_row, 4 if moments else 2)
+        new_first, new_second, mark, direction, *parts = adam_chunk(
+            pieces, gathered, first_moment, second_moment, marks, moments, at, cuts, n_row
         )
         moments, ready = [new_first, new_second], [mark]
-        core = exchange(direction, "row", n_row, 1)
-        for (start, width), part in zip(cuts, parts):
-            chunks.append((at + start, start, [direction, core], over_y(part, n_row)))
-
-    projector = pltpu.with_memory_space_constraint(projector, pltpu.VMEM)
-    each = len(strips) // len(chunks)
-    shape = weight.shape
-    _, start, near, _ = chunks[0]
-    *first_held, mark = weight_update(projector, shape, [], near=near, near_held=held[:each], start=start)
-    held[:each] = first_held
+        here = slice(len(chunks) * each, (len(chunks) + 1) * each)
+        near = [[direction], [exchange(part, "row", n_row, 1) for part in parts]]
+        chunks.append((at, here, near, over_y(direction, n_row)))
+        if len(chunks) > 1:
+            before, part = chunks[-2][1], (0.5, 1)
+            *held[before], mark = weight_update(
+                projector, shape, ready, near=chunks[-2][2], near_held=held[before], part=part
+            )
+            ready = [mark]
+        *held[here], mark = weight_update(
+            projector, shape, ready, near=near, near_held=held[here], part=(0, 0.5)
+        )
+        marks = [mark]
+
     new_weight = []
-    for index, (at, _, _, far) in enumerate(chunks):
-        far = with_core(far, [mark], n_row, 2)
-        here, there = slice(index * each, (index + 1) * each), slice((index + 1) * each, (index + 2) * each)
-        _, start, near, _ = chunks[index + 1] if index + 1 < len(chunks) else (0, 0, (), 0)
-        new, *moved, mark = weight_update(
-            projector, shape, [], far, held[here], at, near, held[there], start, new_weight
+    for index, (at, here, near, far) in enumerate(chunks):
+        far = with_core(far, marks, n_row, 2)
+        if not index:
+            last = chunks[-1][1]
+            *held[last], mark = weight_update(
+                projector, shape, marks, near=chunks[-1][2], near_held=held[last], part=(0.5, 1)
+            )
+            marks = [mark]
+        masks = ()
+        if index and index == len(chunks) - 1:
+            *held[here], mark = weight_update(
+                projector, shape, marks, far[0::2], held[here], masks=range(2, n_row, 2), final=False
+            )
+            marks, far, masks = [mark], far[1::2], range(3, n_row, 2)
+        new, *_, mark = weight_update(
+            projector, shape, marks, far, held[here], at, masks=masks, carried=new_weight
         )
-        new_weight = [new]
-        held[there] = moved[each:]
+        new_weight, marks = [new], [mark]
     return (new_weight[0], *moments)
 
 

time: 74.8 us -> 72.7 us (0.972)
  waiting for transfers between devices: 8.48 us -> 4.35 us
  Pallas kernels: 46.2 us -> 50.1 us
  starting transfers between devices: 18.9 us -> 17 us
    pallas_call x5 -> x7, Pallas kernels: 22.5 us -> 26.9 us  [weight_update(): pl.pallas_call(functools.partial(update_kernel, far_at, height, near_step...]
    ppermute x28, waiting for transfers between devices: 8.48 us -> 4.35 us  [exchange(): return lax.ppermute(values, axis, [(i, i ^ mask) for i in range(size)])]
    ppermute x28, starting transfers between devices: 18.9 us -> 17 us  [exchange(): return lax.ppermute(values, axis, [(i, i ^ mask) for i in range(size)])]
  transfers between devices with their start and end apart: 28 -> 28, of which waited for: 15 -> 7; matrix products, arithmetic and copies ran while one was open for 0% -> 0% of each run, Pallas kernels for 50% -> 53%
where the time goes in v3:
time: 72.7 us; the launch traced here: 72.6 us
  Pallas kernels  50.1 us (69%)
  starting transfers between devices  17 us (23%)
  waiting for transfers between devices  4.35 us (6%)
  between operations  1.07 us (1%)
    pallas_call x7, Pallas kernels, weight_update(): pl.pallas_call(functools.partial(update_kernel, far_at, height, near_step...  26.9 us
    ppermute x28, starting transfers between devices, exchange(): return lax.ppermute(values, axis, [(i, i ^ mask) for i in range(size)])  17 us
    pallas_call x3, Pallas kernels, load_weight(): pl.pallas_call(functools.partial(load_kernel, cuts, height), out_shape=[p...  13.3 us
    pallas_call x2, Pallas kernels, adam_chunk(): pl.pallas_call(functools.partial(adam_kernel, counts, len(pieces), len(ma...  5.2 us
    pallas_call x1, Pallas kernels, lowered_terms(): pl.pallas_call(functools.partial(lowered_kernel, height, cuts), out_shape...  4.41 us
    ppermute x28, waiting for transfers between devices, exchange(): return lax.ppermute(values, axis, [(i, i ^ mask) for i in range(size)])  4.35 us
  transfers between devices with their start and end apart: 28, of which 7 were waited for; matrix products, arithmetic and copies ran while one was open for 0% of the time, Pallas kernels for 53%

profile of v3, /device:TPU:0, one launch (start us, length us, event | category | flops | bytes accessed | tf_op | source)
XLA Modules:
  0.0 72.6 jit_solution(4716360693291118500)
XLA Ops:
  0.6 4.4 %lowered_terms.1 = (f32[128,256]{1,0:T(8,128)S(1)}, bf16[128,256]{1,0:T(8,128)(2,1)S(1)}, bf16[128,256]{1,0:T(8,128)(2,1)S(1)}, bf16[128,256]{1,0:T(8,128)(2,1)S...) custom-call(bf16[128,4096]{1,0:T(8,128)(2,1)} %grad_hbm.1, ...), custom_call_target="tpu_custom_call" | custom-call | flops 1 | bytes 1 | tf_op jit(solution)/shard_map/lowered_terms/pallas_call | solution.py:75
  5.0 0.5 collective-permute-start.7
  5.6 2.6 %collective-permute-start.1 = (bf16[128,256]{1,0:T(8,128)(2,1)S(1)}, bf16[128,256]{1,0:T(8,128)(2,1)S(1)}, u32[]{:S(2)}, u32[]{:S(2)}) collective-permute-start(bf16[128,256]{1,0:T(8,128)(2,1)S(1)} %get-tuple-element.83), channel_id=1, source_target_pairs={{0,16},{8,24},{16,0},{24,8},{1,17},{9,25},{17,1},{25,9},{2,18},{10... | collective-permute-start | bytes 196616 | tf_op jit(solution)/shard_map/ppermute | solution.py:24
  8.4 3.5 %load_weight.3 = (f32[4096,256]{1,0:T(8,128)S(1)}, f32[4096,256]{1,0:T(8,128)S(1)}, bf16[16,128]{1,0:T(8,128)(2,1)S(1)}) custom-call(f32[4096,2048]{1,0:T(8,128)} %weight_hbm.5, bf16[128,256]{1,0:T(8,128)(2,1)S(1)} %get-tuple-element.82.mark_in), custom_call_target="tpu_custom_call" | custom-call | flops 1 | bytes 1 | tf_op jit(solution)/shard_map/load_weight/pallas_call | solution.py:113
  12.2 1.7 %collective-permute-start.9 = (bf16[256,1024]{1,0:T(8,128)(2,1)S(1)}, bf16[256,1024]{1,0:T(8,128)(2,1)S(1)}, u32[]{:S(2)}, u32[]{:S(2)}) collective-permute-start(bf16[256,1024]{1,0:T(8,128)(2,1)S(1)} %get-tuple-element.92.refs_2_), channel_id=1, source_target_pairs={{0,16},{8,24},{16,0},{24,8},{1,17},{9,25},{17,1},{25,9},{2,18},{10... | collective-permute-start | bytes 1572872 | tf_op jit(solution)/shard_map/ppermute | solution.py:24
  14.1 3.7 %collective-permute-start.5 = (bf16[256,128]{1,0:T(8,128)(2,1)S(1)}, bf16[256,128]{1,0:T(8,128)(2,1)S(1)}, u32[]{:S(2)}, u32[]{:S(2)}) collective-permute-start(bf16[256,128]{1,0:T(8,128)(2,1)S(1)} %share_sum.1.mark_in.refs_0_), channel_id=1, source_target_pairs={{0,6},{1,7},{2,4},{3,5},{4,2},{5,3},{6,0},{7,1},{8,14},{9,15},{10,... | collective-permute-start | bytes 196616 | tf_op jit(solution)/shard_map/ppermute | solution.py:24
  17.7 0.8 %collective-permute-start.3 = (bf16[256,128]{1,0:T(8,128)(2,1)S(1)}, bf16[256,128]{1,0:T(8,128)(2,1)S(1)}, u32[]{:S(2)}, u32[]{:S(2)}) collective-permute-start(bf16[256,128]{1,0:T(8,128)(2,1)S(1)} %share_sum.1.mark_in.refs_0_), channel_id=1, source_target_pairs={{0,2},{1,3},{2,0},{3,1},{4,6},{5,7},{6,4},{7,5},{8,10},{9,11},{10,... | collective-permute-start | bytes 196616 | tf_op jit(solution)/shard_map/ppermute | solution.py:24
  18.5 4.8 %load_weight.4 = (f32[4096,256]{1,0:T(8,128)S(1)}, f32[4096,256]{1,0:T(8,128)S(1)}, f32[4096,256]{1,0:T(8,128)S(1)}, bf16[16,128]{1,0:T(8,128)(2,1)S(1)}) custom-call(f32[4096,2048]{1,0:T(8,128)} %weight_hbm.5, bf16[256,128]{1,0:T(8,128)(2,1)S(1)} %share_sum.1.mark_in.refs_0_), custom_call_target="tpu_custom_call" | custom-call | flops 1 | bytes 1 | tf_op jit(solution)/shard_map/load_weight/pallas_call | solution.py:113
  23.4 1.6 %collective-permute-start.6 = (bf16[1024,128]{1,0:T(8,128)(2,1)S(1)}, bf16[1024,128]{1,0:T(8,128)(2,1)S(1)}, u32[]{:S(2)}, u32[]{:S(2)}) collective-permute-start(bf16[1024,128]{1,0:T(8,128)(2,1)S(1)} %get-tuple-element.87.refs_0_), channel_id=1, source_target_pairs={{0,1},{1,0},{2,3},{3,2},{4,5},{5,4},{6,7},{7,6},{8,9},{9,8},{10,11... | collective-permute-start | bytes 786440 | tf_op jit(solution)/shard_map/ppermute | solution.py:24
  25.0 0.5 collective-permute-start.8
  25.5 4.9 %load_weight.5 = (f32[4096,256]{1,0:T(8,128)S(1)}, f32[4096,256]{1,0:T(8,128)S(1)}, f32[4096,256]{1,0:T(8,128)S(1)}, bf16[16,128]{1,0:T(8,128)(2,1)S(1)}) custom-call(f32[4096,2048]{1,0:T(8,128)} %weight_hbm.5, bf16[16,128]{1,0:T(8,128)(2,1)S(1)} %get-tuple-element.93.mark_in), custom_call_target="tpu_custom_call" | custom-call | flops 1 | bytes 1 | tf_op jit(solution)/shard_map/load_weight/pallas_call | solution.py:113
  30.4 1.1 %collective-permute-done.6.refs_1_ = bf16[1024,128]{1,0:T(8,128)(2,1)S(1)} collective-permute-done((bf16[1024,128]{1,0:T(8,128)(2,1)S(1)}, bf16[1024,128]{1,0:T(8,128)(2,1)S(1)}, u32[]{:S(2)}, u32[]{:S(2)}) %collective-permute-start.6) | collective-permute-done | bytes 262176 | tf_op jit(solution)/shard_map/ppermute | solution.py:24
  32.1 1.0 %collective-permute-done.10.refs_5_ = bf16[256,512]{1,0:T(8,128)(2,1)S(1)} collective-permute-done((bf16[256,512]{1,0:T(8,128)(2,1)S(1)}, bf16[256,512]{1,0:T(8,128)(2,1)S(1)}, u32[]{:S(2)}, u32[]{:S(2)}) %collective-permute-start.10) | collective-permute-done | bytes 262176 | tf_op jit(solution)/shard_map/ppermute | solution.py:24
  33.6 2.6 %adam_chunk.2 = (f32[256,2048]{1,0:T(8,128)}, f32[256,2048]{1,0:T(8,128)}, bf16[16,128]{1,0:T(8,128)(2,1)S(1)}, bf16[256,1024]{1,0:T(8,128)(2,1)S(1)}, bf16[256,...) custom-call(bf16[1024,128]{1,0:T(8,128)(2,1)S(1)} %get-tuple-element.87.refs_0_, ...), custom_call_target="tpu_custom_call" | custom-call | flops 1 | bytes 1 | tf_op jit(solution)/shard_map/adam_chunk/pallas_call | solution.py:224
  37.2 1.2 %collective-permute-done.8.refs_0_ = bf16[256,1024]{1,0:T(8,128)(2,1)S(1)} collective-permute-done((bf16[256,1024]{1,0:T(8,128)(2,1)S(1)}, bf16[256,1024]{1,0:T(8,128)(2,1)S(1)}, u32[]{:S(2)}, u32[]{:S(2)}) %collective-permute-start.8) | collective-permute-done | bytes 524320 | tf_op jit(solution)/shard_map/ppermute | solution.py:24
  39.5 2.6 %weight_update.7 = (f32[4096,256]{1,0:T(8,128)S(1)}, f32[4096,256]{1,0:T(8,128)S(1)}, f32[4096,256]{1,0:T(8,128)S(1)}, f32[4096,256]{1,0:T(8,128)S(1)}, bf16[16,128]{1,0:T(8,128)(2,1)S(1)}) custom-call(bf16[4096,1024]{1,0:T(8,128)(2,1)S(1)} %bitcast.1, ...), custom_call_target="tpu_custom_call", output_to_operand_aliasing={{0}: (4, {}), {1}: (5, {}), {2}: (6, {}), {3}: (7, {})} | custom-call | flops 1 | bytes 1 | tf_op jit(solution)/shard_map/weight_update/pallas_call | solution.py:324
  42.1 2.6 %adam_chunk.3 = (f32[256,2048]{1,0:T(8,128)}, f32[256,2048]{1,0:T(8,128)}, bf16[16,128]{1,0:T(8,128)(2,1)S(1)}, bf16[256,1024]{1,0:T(8,128)(2,1)S(1)}, bf16[256,...) custom-call(bf16[1024,128]{1,0:T(8,128)(2,1)S(1)} %get-tuple-element, ...), custom_call_target="tpu_custom_call", output_to_operand_aliasing={{0}: (12, {}), {1}: (13, {})} | custom-call | flops 1 | bytes 1 | tf_op jit(solution)/shard_map/adam_chunk/pallas_call | solution.py:224
  44.9 0.8 %collective-permute-start.18 = (bf16[256,1024]{1,0:T(8,128)(2,1)S(1)}, bf16[256,1024]{1,0:T(8,128)(2,1)S(1)}, u32[]{:S(2)}, u32[]{:S(2)}) collective-permute-start(bf16[256,1024]{1,0:T(8,128)(2,1)S(1)} %get-tuple-element.114.refs_0_), channel_id=1, source_target_pairs={{0,16},{8,24},{16,0},{24,8},{1,17},{9,25},{17,1},{25,9},{2,18},{10... | collective-permute-start | bytes 1572872 | tf_op jit(solution)/shard_map/ppermute | solution.py:24
  46.4 2.6 %weight_update.8 = (f32[4096,256]{1,0:T(8,128)S(1)}, f32[4096,256]{1,0:T(8,128)S(1)}, f32[4096,256]{1,0:T(8,128)S(1)}, f32[4096,256]{1,0:T(8,128)S(1)}, bf16[16,128]{1,0:T(8,128)(2,1)S(1)}) custom-call(bf16[4096,1024]{1,0:T(8,128)(2,1)S(1)} %bitcast.1, ...), custom_call_target="tpu_custom_call", output_to_operand_aliasing={{0}: (4, {}), {1}: (5, {}), {2}: (6, {}), {3}: (7, {})} | custom-call | flops 1 | bytes 1 | tf_op jit(solution)/shard_map/weight_update/pallas_call | solution.py:324
  49.0 2.8 %weight_update.9 = (f32[4096,256]{1,0:T(8,128)S(1)}, f32[4096,256]{1,0:T(8,128)S(1)}, f32[4096,256]{1,0:T(8,128)S(1)}, f32[4096,256]{1,0:T(8,128)S(1)}, bf16[16,128]{1,0:T(8,128)(2,1)S(1)}) custom-call(bf16[4096,1024]{1,0:T(8,128)(2,1)S(1)} %bitcast.1, ...), custom_call_target="tpu_custom_call", output_to_operand_aliasing={{0}: (6, {}), {1}: (7, {}), {2}: (8, {}), {3}: (9, {})} | custom-call | flops 1 | bytes 1 | tf_op jit(solution)/shard_map/weight_update/pallas_call | solution.py:324
  52.4 2.6 %weight_update.10 = (f32[4096,256]{1,0:T(8,128)S(1)}, f32[4096,256]{1,0:T(8,128)S(1)}, f32[4096,256]{1,0:T(8,128)S(1)}, f32[4096,256]{1,0:T(8,128)S(1)}, bf16[16,128]{1,0:T(8,128)(2,1)S(1)}) custom-call(bf16[4096,1024]{1,0:T(8,128)(2,1)S(1)} %bitcast.1, ...), custom_call_target="tpu_custom_call", output_to_operand_aliasing={{0}: (6, {}), {1}: (7, {}), {2}: (8, {}), {3}: (9, {})} | custom-call | flops 1 | bytes 1 | tf_op jit(solution)/shard_map/weight_update/pallas_call | solution.py:324
  55.0 6.6 %weight_update.11 = (f32[4096,2048]{1,0:T(8,128)}, f32[4096,256]{1,0:T(8,128)S(1)}, f32[4096,256]{1,0:T(8,128)S(1)}, f32[4096,256]{1,0:T(8,128)S(1)}, f32[4096,2...) custom-call(bf16[4096,1024]{1,0:T(8,128)(2,1)S(1)} %bitcast.1, ...), custom_call_target="tpu_custom_call", output_to_operand_aliasing={{1}: (4, {}), {2}: (5, {}), {3}: (6, {}), {4}: (7, {})} | custom-call | flops 1 | bytes 1 | tf_op jit(solution)/shard_map/weight_update/pallas_call | solution.py:324
  62.6 2.8 %weight_update.12 = (f32[4096,256]{1,0:T(8,128)S(1)}, f32[4096,256]{1,0:T(8,128)S(1)}, f32[4096,256]{1,0:T(8,128)S(1)}, f32[4096,256]{1,0:T(8,128)S(1)}, bf16[16,128]{1,0:T(8,128)(2,1)S(1)}) custom-call(bf16[4096,1024]{1,0:T(8,128)(2,1)S(1)} %bitcast.1, ...), custom_call_target="tpu_custom_call", output_to_operand_aliasing={{0}: (2, {}), {1}: (3, {}), {2}: (4, {}), {3}: (5, {})} | custom-call | flops 1 | bytes 1 | tf_op jit(solution)/shard_map/weight_update/pallas_call | solution.py:324
  65.4 7.0 %weight_update.13 = (f32[4096,2048]{1,0:T(8,128)}, f32[4096,256]{1,0:T(8,128)S(1)}, f32[4096,256]{1,0:T(8,128)S(1)}, f32[4096,256]{1,0:T(8,128)S(1)}, f32[4096,256]{1,0:T(8,128)S(1)}, /*index=5*/bf16[16,128]{1,0:T(8,128)(2,1)}) custom-call(bf16[4096,1024]{1,0:T(8,128)(2,1)S(1)} %bitcast.1, ...), custom_call_target="tpu_custom_call", output_to_operand_aliasing={{1}: (3, {}), {2}: (4, {}), {3}: (5, {}), {4}: (6, {}), {0}... | custom-call | flops 1 | bytes 1 | tf_op jit(solution)/shard_map/weight_update/pallas_call | solution.py:324
  (61 shorter events, 6.2 us)
Async XLA Ops:
  5.0 28.5 %collective-permute-start.7 = (bf16[256,2048]{1,0:T(8,128)(2,1)S(1)}, bf16[256,2048]{1,0:T(8,128)(2,1)S(1)}, u32[]{:S(2)}, u32[]{:S(2)}) collective-permute-start(bf16[256,2048]{1,0:T(8,128)(2,1)S(1)} %get-tuple-element.91), channel_id=1, source_target_pairs={{0,8},{8,0},{16,24},{24,16},{1,9},{9,1},{17,25},{25,17},{2,10},{10... | collective-permute-start | bytes 3145736 | tf_op jit(solution)/shard_map/ppermute | solution.py:24
  5.6 6.3 %collective-permute-start.1 = (bf16[128,256]{1,0:T(8,128)(2,1)S(1)}, bf16[128,256]{1,0:T(8,128)(2,1)S(1)}, u32[]{:S(2)}, u32[]{:S(2)}) collective-permute-start(bf16[128,256]{1,0:T(8,128)(2,1)S(1)} %get-tuple-element.83), channel_id=1, source_target_pairs={{0,16},{8,24},{16,0},{24,8},{1,17},{9,25},{17,1},{25,9},{2,18},{10... | collective-permute-start | bytes 196616 | tf_op jit(solution)/shard_map/ppermute | solution.py:24
  8.2 4.0 %collective-permute-start.2 = (bf16[128,256]{1,0:T(8,128)(2,1)S(1)}, bf16[128,256]{1,0:T(8,128)(2,1)S(1)}, u32[]{:S(2)}, u32[]{:S(2)}) collective-permute-start(bf16[128,256]{1,0:T(8,128)(2,1)S(1)} %get-tuple-element.84), channel_id=1, source_target_pairs={{0,24},{8,16},{16,8},{24,0},{1,25},{9,17},{17,9},{25,1},{2,26},{10... | collective-permute-start | bytes 196616 | tf_op jit(solution)/shard_map/ppermute | solution.py:24
  8.2 4.0 %collective-permute-start = (bf16[128,256]{1,0:T(8,128)(2,1)S(1)}, bf16[128,256]{1,0:T(8,128)(2,1)S(1)}, u32[]{:S(2)}, u32[]{:S(2)}) collective-permute-start(bf16[128,256]{1,0:T(8,128)(2,1)S(1)} %get-tuple-element.82.mark_in), channel_id=1, source_target_pairs={{0,8},{8,0},{16,24},{24,16},{1,9},{9,1},{17,25},{25,17},{2,10},{10... | collective-permute-start | bytes 196616 | tf_op jit(solution)/shard_map/ppermute | solution.py:24
  12.2 19.3 %collective-permute-start.9 = (bf16[256,1024]{1,0:T(8,128)(2,1)S(1)}, bf16[256,1024]{1,0:T(8,128)(2,1)S(1)}, u32[]{:S(2)}, u32[]{:S(2)}) collective-permute-start(bf16[256,1024]{1,0:T(8,128)(2,1)S(1)} %get-tuple-element.92.refs_2_), channel_id=1, source_target_pairs={{0,16},{8,24},{16,0},{24,8},{1,17},{9,25},{17,1},{25,9},{2,18},{10... | collective-permute-start | bytes 1572872 | tf_op jit(solution)/shard_map/ppermute | solution.py:24
  14.1 9.3 %collective-permute-start.5 = (bf16[256,128]{1,0:T(8,128)(2,1)S(1)}, bf16[256,128]{1,0:T(8,128)(2,1)S(1)}, u32[]{:S(2)}, u32[]{:S(2)}) collective-permute-start(bf16[256,128]{1,0:T(8,128)(2,1)S(1)} %share_sum.1.mark_in.refs_0_), channel_id=1, source_target_pairs={{0,6},{1,7},{2,4},{3,5},{4,2},{5,3},{6,0},{7,1},{8,14},{9,15},{10,... | collective-permute-start | bytes 196616 | tf_op jit(solution)/shard_map/ppermute | solution.py:24
  17.7 5.7 %collective-permute-start.4 = (bf16[256,128]{1,0:T(8,128)(2,1)S(1)}, bf16[256,128]{1,0:T(8,128)(2,1)S(1)}, u32[]{:S(2)}, u32[]{:S(2)}) collective-permute-start(bf16[256,128]{1,0:T(8,128)(2,1)S(1)} %share_sum.1.mark_in.refs_0_), channel_id=1, source_target_pairs={{0,4},{1,5},{2,6},{3,7},{4,0},{5,1},{6,2},{7,3},{8,12},{9,13},{10,... | collective-permute-start | bytes 196616 | tf_op jit(solution)/shard_map/ppermute | solution.py:24
  17.7 5.7 %collective-permute-start.3 = (bf16[256,128]{1,0:T(8,128)(2,1)S(1)}, bf16[256,128]{1,0:T(8,128)(2,1)S(1)}, u32[]{:S(2)}, u32[]{:S(2)}) collective-permute-start(bf16[256,128]{1,0:T(8,128)(2,1)S(1)} %share_sum.1.mark_in.refs_0_), channel_id=1, source_target_pairs={{0,2},{1,3},{2,0},{3,1},{4,6},{5,7},{6,4},{7,5},{8,10},{9,11},{10,... | collective-permute-start | bytes 196616 | tf_op jit(solution)/shard_map/ppermute | solution.py:24
  23.4 8.1 %collective-permute-start.6 = (bf16[1024,128]{1,0:T(8,128)(2,1)S(1)}, bf16[1024,128]{1,0:T(8,128)(2,1)S(1)}, u32[]{:S(2)}, u32[]{:S(2)}) collective-permute-start(bf16[1024,128]{1,0:T(8,128)(2,1)S(1)} %get-tuple-element.87.refs_0_), channel_id=1, source_target_pairs={{0,1},{1,0},{2,3},{3,2},{4,5},{5,4},{6,7},{7,6},{8,9},{9,8},{10,11... | collective-permute-start | bytes 786440 | tf_op jit(solution)/shard_map/ppermute | solution.py:24
  25.0 13.4 %collective-permute-start.8 = (bf16[256,1024]{1,0:T(8,128)(2,1)S(1)}, bf16[256,1024]{1,0:T(8,128)(2,1)S(1)}, u32[]{:S(2)}, u32[]{:S(2)}) collective-permute-start(bf16[256,1024]{1,0:T(8,128)(2,1)S(1)} %get-tuple-element.90.refs_2_), channel_id=1, source_target_pairs={{0,16},{8,24},{16,0},{24,8},{1,17},{9,25},{17,1},{25,9},{2,18},{10... | collective-permute-start | bytes 1572872 | tf_op jit(solution)/shard_map/ppermute | solution.py:24
  36.2 2.8 %collective-permute-start.16 = (bf16[256,512]{1,0:T(8,128)(2,1)S(1)}, bf16[256,512]{1,0:T(8,128)(2,1)S(1)}, u32[]{:S(2)}, u32[]{:S(2)}) collective-permute-start(bf16[256,512]{1,0:T(8,128)(2,1)S(1)} %get-tuple-element.105), channel_id=1, source_target_pairs={{0,8},{8,0},{16,24},{24,16},{1,9},{9,1},{17,25},{25,17},{2,10},{10... | collective-permute-start | bytes 786440 | tf_op jit(solution)/shard_map/ppermute | solution.py:24
  36.7 15.1 %collective-permute-start.19 = (bf16[256,1024]{1,0:T(8,128)(2,1)S(1)}, bf16[256,1024]{1,0:T(8,128)(2,1)S(1)}, u32[]{:S(2)}, u32[]{:S(2)}) collective-permute-start(bf16[256,1024]{1,0:T(8,128)(2,1)S(1)} %get-tuple-element.104.refs_0_), channel_id=1, source_target_pairs={{0,16},{8,24},{16,0},{24,8},{1,17},{9,25},{17,1},{25,9},{2,18},{10... | collective-permute-start | bytes 1572872 | tf_op jit(solution)/shard_map/ppermute | solution.py:24
  38.4 3.7 %collective-permute-start.12 = (bf16[256,256]{1,0:T(8,128)(2,1)S(1)}, bf16[256,256]{1,0:T(8,128)(2,1)S(1)}, u32[]{:S(2)}, u32[]{:S(2)}) collective-permute-start(bf16[256,256]{1,0:T(8,128)(2,1)S(1)} %get-tuple-element.100), channel_id=1, source_target_pairs={{0,8},{8,0},{16,24},{24,16},{1,9},{9,1},{17,25},{25,17},{2,10},{10... | collective-permute-start | bytes 393224 | tf_op jit(solution)/shard_map/ppermute | solution.py:24
  38.5 3.6 %collective-permute-start.13 = (bf16[256,256]{1,0:T(8,128)(2,1)S(1)}, bf16[256,256]{1,0:T(8,128)(2,1)S(1)}, u32[]{:S(2)}, u32[]{:S(2)}) collective-permute-start(bf16[256,256]{1,0:T(8,128)(2,1)S(1)} %get-tuple-element.101), channel_id=1, source_target_pairs={{0,8},{8,0},{16,24},{24,16},{1,9},{9,1},{17,25},{25,17},{2,10},{10... | collective-permute-start | bytes 393224 | tf_op jit(solution)/shard_map/ppermute | solution.py:24
  39.0 3.1 %collective-permute-start.14 = (bf16[256,256]{1,0:T(8,128)(2,1)S(1)}, bf16[256,256]{1,0:T(8,128)(2,1)S(1)}, u32[]{:S(2)}, u32[]{:S(2)}) collective-permute-start(bf16[256,256]{1,0:T(8,128)(2,1)S(1)} %get-tuple-element.102), channel_id=1, source_target_pairs={{0,8},{8,0},{16,24},{24,16},{1,9},{9,1},{17,25},{25,17},{2,10},{10... | collective-permute-start | bytes 393224 | tf_op jit(solution)/shard_map/ppermute | solution.py:24
  39.1 3.0 %collective-permute-start.15 = (bf16[256,256]{1,0:T(8,128)(2,1)S(1)}, bf16[256,256]{1,0:T(8,128)(2,1)S(1)}, u32[]{:S(2)}, u32[]{:S(2)}) collective-permute-start(bf16[256,256]{1,0:T(8,128)(2,1)S(1)} %get-tuple-element.103), channel_id=1, source_target_pairs={{0,8},{8,0},{16,24},{24,16},{1,9},{9,1},{17,25},{25,17},{2,10},{10... | collective-permute-start | bytes 393224 | tf_op jit(solution)/shard_map/ppermute | solution.py:24
  44.9 17.1 %collective-permute-start.18 = (bf16[256,1024]{1,0:T(8,128)(2,1)S(1)}, bf16[256,1024]{1,0:T(8,128)(2,1)S(1)}, u32[]{:S(2)}, u32[]{:S(2)}) collective-permute-start(bf16[256,1024]{1,0:T(8,128)(2,1)S(1)} %get-tuple-element.114.refs_0_), channel_id=1, source_target_pairs={{0,16},{8,24},{16,0},{24,8},{1,17},{9,25},{17,1},{25,9},{2,18},{10... | collective-permute-start | bytes 1572872 | tf_op jit(solution)/shard_map/ppermute | solution.py:24
  45.7 3.3 %collective-permute-start.21 = (bf16[256,256]{1,0:T(8,128)(2,1)S(1)}, bf16[256,256]{1,0:T(8,128)(2,1)S(1)}, u32[]{:S(2)}, u32[]{:S(2)}) collective-permute-start(bf16[256,256]{1,0:T(8,128)(2,1)S(1)} %get-tuple-element.116), channel_id=1, source_target_pairs={{0,8},{8,0},{16,24},{24,16},{1,9},{9,1},{17,25},{25,17},{2,10},{10... | collective-permute-start | bytes 393224 | tf_op jit(solution)/shard_map/ppermute | solution.py:24
  45.9 3.1 %collective-permute-start.22 = (bf16[256,256]{1,0:T(8,128)(2,1)S(1)}, bf16[256,256]{1,0:T(8,128)(2,1)S(1)}, u32[]{:S(2)}, u32[]{:S(2)}) collective-permute-start(bf16[256,256]{1,0:T(8,128)(2,1)S(1)} %get-tuple-element.117), channel_id=1, source_target_pairs={{0,8},{8,0},{16,24},{24,16},{1,9},{9,1},{17,25},{25,17},{2,10},{10... | collective-permute-start | bytes 393224 | tf_op jit(solution)/shard_map/ppermute | solution.py:24
  46.2 2.8 %collective-permute-start.23 = (bf16[256,256]{1,0:T(8,128)(2,1)S(1)}, bf16[256,256]{1,0:T(8,128)(2,1)S(1)}, u32[]{:S(2)}, u32[]{:S(2)}) collective-permute-start(bf16[256,256]{1,0:T(8,128)(2,1)S(1)} %get-tuple-element.118), channel_id=1, source_target_pairs={{0,8},{8,0},{16,24},{24,16},{1,9},{9,1},{17,25},{25,17},{2,10},{10... | collective-permute-start | bytes 393224 | tf_op jit(solution)/shard_map/ppermute | solution.py:24
  51.9 3.2 %collective-permute-start.24 = (bf16[256,512]{1,0:T(8,128)(2,1)S(1)}, bf16[256,512]{1,0:T(8,128)(2,1)S(1)}, u32[]{:S(2)}, u32[]{:S(2)}) collective-permute-start(bf16[256,512]{1,0:T(8,128)(2,1)S(1)} %get-tuple-element.131), channel_id=1, source_target_pairs={{0,8},{8,0},{16,24},{24,16},{1,9},{9,1},{17,25},{25,17},{2,10},{10... | collective-permute-start | bytes 786440 | tf_op jit(solution)/shard_map/ppermute | solution.py:24
  52.3 2.8 %collective-permute-start.25 = (bf16[256,512]{1,0:T(8,128)(2,1)S(1)}, bf16[256,512]{1,0:T(8,128)(2,1)S(1)}, u32[]{:S(2)}, u32[]{:S(2)}) collective-permute-start(bf16[256,512]{1,0:T(8,128)(2,1)S(1)} %get-tuple-element.132), channel_id=1, source_target_pairs={{0,8},{8,0},{16,24},{24,16},{1,9},{9,1},{17,25},{25,17},{2,10},{10... | collective-permute-start | bytes 786440 | tf_op jit(solution)/shard_map/ppermute | solution.py:24
  62.0 3.4 %collective-permute-start.26 = (bf16[256,512]{1,0:T(8,128)(2,1)S(1)}, bf16[256,512]{1,0:T(8,128)(2,1)S(1)}, u32[]{:S(2)}, u32[]{:S(2)}) collective-permute-start(bf16[256,512]{1,0:T(8,128)(2,1)S(1)} %get-tuple-element.143), channel_id=1, source_target_pairs={{0,8},{8,0},{16,24},{24,16},{1,9},{9,1},{17,25},{25,17},{2,10},{10... | collective-permute-start | bytes 786440 | tf_op jit(solution)/shard_map/ppermute | solution.py:24
  62.1 3.3 %collective-permute-start.27 = (bf16[256,512]{1,0:T(8,128)(2,1)S(1)}, bf16[256,512]{1,0:T(8,128)(2,1)S(1)}, u32[]{:S(2)}, u32[]{:S(2)}) collective-permute-start(bf16[256,512]{1,0:T(8,128)(2,1)S(1)} %get-tuple-element.144), channel_id=1, source_target_pairs={{0,8},{8,0},{16,24},{24,16},{1,9},{9,1},{17,25},{25,17},{2,10},{10... | collective-permute-start | bytes 786440 | tf_op jit(solution)/shard_map/ppermute | solution.py:24
  (8 other events, 51.9 us)

commit v4 on v3

--- a/solution.py
+++ b/solution.py
@@ -254,7 +254,7 @@
             pair[rows, index * span : (index + 1) * span] = piece[...]
 
 
-def update_kernel(far_at, height, near_steps, masks, final, counts, n_near, n_far_held, n_near_held, n_skip, basis_ref, *refs):
+def update_kernel(far_at, height, steps, late, masks, final, counts, n_near, n_far_held, n_near_held, n_skip, basis_ref, *refs):
     far_parts = []
     for count in counts:
         far_parts.append(refs[:count])
@@ -289,15 +289,15 @@
             terms.append((chip ^ (index // 2 + 1), 2 * ranks, pairs.at[index // 2 + 1]))
     if n_near:
         gather_pair(pairs.at[0], near_parts)
-    for step in range(count if far_parts else 0):
+    for step in (range(count) if final else steps if far_parts else ()):
         rows = slice(step * height, (step + 1) * height)
-        for first, depth, pair in terms:
+        for first, depth, pair in terms[late if step in steps else 0 :]:
             subtract(rows, held_refs[:n_far_held], first, depth, pair[...])
         for index, held in enumerate(held_refs[:n_far_held] if final else ()):
             target = outs[0].at[rows, far_at + index * span : far_at + (index + 1) * span]
             copies.append(pltpu.make_async_copy(held.at[rows], target, sems.at[step, index]))
             copies[-1].start()
-    for step in near_steps:
+    for step in steps if n_near else ():
         rows = slice(step * height, (step + 1) * height)
         subtract(rows, held_refs[n_far_held:], chip, 2 * ranks, pairs[0])
     mark_ref[...] = jnp.zeros_like(mark_ref)
@@ -305,7 +305,7 @@
         copy.wait()
 
 
-def weight_update(projector, shape, marks, far=(), far_held=(), far_at=0, near=(), near_held=(), part=(0, 1), masks=(), final=True, carried=()):
+def weight_update(projector, shape, marks, far=(), far_held=(), far_at=0, near=(), near_held=(), part=(0, 1), masks=(), late=0, final=True, carried=()):
     helds = [*far_held, *near_held]
     counts = [len(pieces) for pieces in [*near, *far]]
     flat = sum([*near, *far], [])
@@ -313,7 +313,7 @@
     ranks, width = flat[0].shape[0], span * max(len(far_held), len(near_held))
     height = min(512, rows)
     begin, end = (int(edge * (rows // height)) for edge in part)
-    near_steps = range(begin, end) if near else ()
+    steps = range(begin, end)
     n_plain = 1 + len(flat)
     final = final and bool(far)
     out_shape = [jax.ShapeDtypeStruct(shape, jnp.float32)] if final else []
@@ -323,7 +323,7 @@
     n_skip = len(marks) + len(carried)
     return pl.pallas_call(
         functools.partial(
-            update_kernel, far_at, height, near_steps, masks, final, counts, len(near), len(far_held), len(near_held), n_skip
+            update_kernel, far_at, height, steps, late, masks, final, counts, len(near), len(far_held), len(near_held), n_skip
         ),
         out_shape=out_shape + [pltpu.VMEM(held.shape, jnp.float32) for held in helds] + [MARK],
         in_specs=[VMEM] * (n_plain + len(helds) + len(marks)) + [ANY] * len(carried),
@@ -455,14 +455,16 @@
                 projector, shape, marks, near=chunks[-1][2], near_held=held[last], part=(0.5, 1)
             )
             marks = [mark]
-        masks = ()
+        masks, late = (), 0
         if index and index == len(chunks) - 1:
+            first, second = range(2, n_row, 2), range(3, n_row, 2)
             *held[here], mark = weight_update(
-                projector, shape, marks, far[0::2], held[here], masks=range(2, n_row, 2), final=False
+                projector, shape, marks, far[0::2], held[here], part=(0, 0.5), masks=first, final=False
             )
-            marks, far, masks = [mark], far[1::2], range(3, n_row, 2)
+            marks, far, masks, late = [mark], far[0::2] + far[1::2], [*first, *second], len(first)
         new, *_, mark = weight_update(
-            projector, shape, marks, far, held[here], at, masks=masks, carried=new_weight
+            projector, shape, marks, far, held[here], at,
+            part=(0, 0.5), masks=masks, late=late, carried=new_weight,
         )
         new_weight, marks = [new], [mark]
     return (new_weight[0], *moments)

time: 72.7 us -> 71.5 us (0.983)
  Pallas kernels: 50.1 us -> 48.9 us
    pallas_call x7, Pallas kernels: 26.9 us -> 25.7 us  [weight_update(): pl.pallas_call(functools.partial(update_kernel, far_at, height, steps, la...]
  transfers between devices with their start and end apart: 28 -> 28, of which waited for: 7 -> 7; matrix products, arithmetic and copies ran while one was open for 0% -> 0% of each run, Pallas kernels for 53% -> 52%
where the time goes in v4:
time: 71.5 us; the launch traced here: 71.4 us
  Pallas kernels  48.9 us (68%)
  starting transfers between devices  17 us (24%)
  waiting for transfers between devices  4.35 us (6%)
  between operations  1.07 us (1%)
    pallas_call x7, Pallas kernels, weight_update(): pl.pallas_call(functools.partial(update_kernel, far_at, height, steps, la...  25.7 us
    ppermute x28, starting transfers between devices, exchange(): return lax.ppermute(values, axis, [(i, i ^ mask) for i in range(size)])  17 us
    pallas_call x3, Pallas kernels, load_weight(): pl.pallas_call(functools.partial(load_kernel, cuts, height), out_shape=[p...  13.3 us
    pallas_call x2, Pallas kernels, adam_chunk(): pl.pallas_call(functools.partial(adam_kernel, counts, len(pieces), len(ma...  5.2 us
    pallas_call x1, Pallas kernels, lowered_terms(): pl.pallas_call(functools.partial(lowered_kernel, height, cuts), out_shape...  4.41 us
    ppermute x28, waiting for transfers between devices, exchange(): return lax.ppermute(values, axis, [(i, i ^ mask) for i in range(size)])  4.35 us
  transfers between devices with their start and end apart: 28, of which 7 were waited for; matrix products, arithmetic and copies ran while one was open for 0% of the time, Pallas kernels for 52%

profile of v4, /device:TPU:0, one launch (start us, length us, event | category | flops | bytes accessed | tf_op | source)
XLA Modules:
  0.0 71.4 jit_solution(3470055424221679094)
XLA Ops:
  0.6 4.4 %lowered_terms.1 = (f32[128,256]{1,0:T(8,128)S(1)}, bf16[128,256]{1,0:T(8,128)(2,1)S(1)}, bf16[128,256]{1,0:T(8,128)(2,1)S(1)}, bf16[128,256]{1,0:T(8,128)(2,1)S...) custom-call(bf16[128,4096]{1,0:T(8,128)(2,1)} %grad_hbm.1, ...), custom_call_target="tpu_custom_call" | custom-call | flops 1 | bytes 1 | tf_op jit(solution)/shard_map/lowered_terms/pallas_call | solution.py:75
  5.0 0.5 collective-permute-start.7
  5.6 2.6 %collective-permute-start.1 = (bf16[128,256]{1,0:T(8,128)(2,1)S(1)}, bf16[128,256]{1,0:T(8,128)(2,1)S(1)}, u32[]{:S(2)}, u32[]{:S(2)}) collective-permute-start(bf16[128,256]{1,0:T(8,128)(2,1)S(1)} %get-tuple-element.83), channel_id=1, source_target_pairs={{0,16},{8,24},{16,0},{24,8},{1,17},{9,25},{17,1},{25,9},{2,18},{10... | collective-permute-start | bytes 196616 | tf_op jit(solution)/shard_map/ppermute | solution.py:24
  8.4 3.5 %load_weight.3 = (f32[4096,256]{1,0:T(8,128)S(1)}, f32[4096,256]{1,0:T(8,128)S(1)}, bf16[16,128]{1,0:T(8,128)(2,1)S(1)}) custom-call(f32[4096,2048]{1,0:T(8,128)} %weight_hbm.5, bf16[128,256]{1,0:T(8,128)(2,1)S(1)} %get-tuple-element.82.mark_in), custom_call_target="tpu_custom_call" | custom-call | flops 1 | bytes 1 | tf_op jit(solution)/shard_map/load_weight/pallas_call | solution.py:113
  12.2 1.7 %collective-permute-start.9 = (bf16[256,1024]{1,0:T(8,128)(2,1)S(1)}, bf16[256,1024]{1,0:T(8,128)(2,1)S(1)}, u32[]{:S(2)}, u32[]{:S(2)}) collective-permute-start(bf16[256,1024]{1,0:T(8,128)(2,1)S(1)} %get-tuple-element.92.refs_2_), channel_id=1, source_target_pairs={{0,16},{8,24},{16,0},{24,8},{1,17},{9,25},{17,1},{25,9},{2,18},{10... | collective-permute-start | bytes 1572872 | tf_op jit(solution)/shard_map/ppermute | solution.py:24
  14.1 3.7 %collective-permute-start.5 = (bf16[256,128]{1,0:T(8,128)(2,1)S(1)}, bf16[256,128]{1,0:T(8,128)(2,1)S(1)}, u32[]{:S(2)}, u32[]{:S(2)}) collective-permute-start(bf16[256,128]{1,0:T(8,128)(2,1)S(1)} %share_sum.1.mark_in.refs_0_), channel_id=1, source_target_pairs={{0,6},{1,7},{2,4},{3,5},{4,2},{5,3},{6,0},{7,1},{8,14},{9,15},{10,... | collective-permute-start | bytes 196616 | tf_op jit(solution)/shard_map/ppermute | solution.py:24
  17.7 0.8 %collective-permute-start.3 = (bf16[256,128]{1,0:T(8,128)(2,1)S(1)}, bf16[256,128]{1,0:T(8,128)(2,1)S(1)}, u32[]{:S(2)}, u32[]{:S(2)}) collective-permute-start(bf16[256,128]{1,0:T(8,128)(2,1)S(1)} %share_sum.1.mark_in.refs_0_), channel_id=1, source_target_pairs={{0,2},{1,3},{2,0},{3,1},{4,6},{5,7},{6,4},{7,5},{8,10},{9,11},{10,... | collective-permute-start | bytes 196616 | tf_op jit(solution)/shard_map/ppermute | solution.py:24
  18.5 4.8 %load_weight.4 = (f32[4096,256]{1,0:T(8,128)S(1)}, f32[4096,256]{1,0:T(8,128)S(1)}, f32[4096,256]{1,0:T(8,128)S(1)}, bf16[16,128]{1,0:T(8,128)(2,1)S(1)}) custom-call(f32[4096,2048]{1,0:T(8,128)} %weight_hbm.5, bf16[256,128]{1,0:T(8,128)(2,1)S(1)} %share_sum.1.mark_in.refs_0_), custom_call_target="tpu_custom_call" | custom-call | flops 1 | bytes 1 | tf_op jit(solution)/shard_map/load_weight/pallas_call | solution.py:113
  23.4 1.6 %collective-permute-start.6 = (bf16[1024,128]{1,0:T(8,128)(2,1)S(1)}, bf16[1024,128]{1,0:T(8,128)(2,1)S(1)}, u32[]{:S(2)}, u32[]{:S(2)}) collective-permute-start(bf16[1024,128]{1,0:T(8,128)(2,1)S(1)} %get-tuple-element.87.refs_0_), channel_id=1, source_target_pairs={{0,1},{1,0},{2,3},{3,2},{4,5},{5,4},{6,7},{7,6},{8,9},{9,8},{10,11... | collective-permute-start | bytes 786440 | tf_op jit(solution)/shard_map/ppermute | solution.py:24
  25.0 0.5 collective-permute-start.8
  25.5 4.9 %load_weight.5 = (f32[4096,256]{1,0:T(8,128)S(1)}, f32[4096,256]{1,0:T(8,128)S(1)}, f32[4096,256]{1,0:T(8,128)S(1)}, bf16[16,128]{1,0:T(8,128)(2,1)S(1)}) custom-call(f32[4096,2048]{1,0:T(8,128)} %weight_hbm.5, bf16[16,128]{1,0:T(8,128)(2,1)S(1)} %get-tuple-element.93.mark_in), custom_call_target="tpu_custom_call" | custom-call | flops 1 | bytes 1 | tf_op jit(solution)/shard_map/load_weight/pallas_call | solution.py:113
  30.4 1.1 %collective-permute-done.6.refs_1_ = bf16[1024,128]{1,0:T(8,128)(2,1)S(1)} collective-permute-done((bf16[1024,128]{1,0:T(8,128)(2,1)S(1)}, bf16[1024,128]{1,0:T(8,128)(2,1)S(1)}, u32[]{:S(2)}, u32[]{:S(2)}) %collective-permute-start.6) | collective-permute-done | bytes 262176 | tf_op jit(solution)/shard_map/ppermute | solution.py:24
  32.1 1.0 %collective-permute-done.10.refs_5_ = bf16[256,512]{1,0:T(8,128)(2,1)S(1)} collective-permute-done((bf16[256,512]{1,0:T(8,128)(2,1)S(1)}, bf16[256,512]{1,0:T(8,128)(2,1)S(1)}, u32[]{:S(2)}, u32[]{:S(2)}) %collective-permute-start.10) | collective-permute-done | bytes 262176 | tf_op jit(solution)/shard_map/ppermute | solution.py:24
  33.6 2.6 %adam_chunk.2 = (f32[256,2048]{1,0:T(8,128)}, f32[256,2048]{1,0:T(8,128)}, bf16[16,128]{1,0:T(8,128)(2,1)S(1)}, bf16[256,1024]{1,0:T(8,128)(2,1)S(1)}, bf16[256,...) custom-call(bf16[1024,128]{1,0:T(8,128)(2,1)S(1)} %get-tuple-element.87.refs_0_, ...), custom_call_target="tpu_custom_call" | custom-call | flops 1 | bytes 1 | tf_op jit(solution)/shard_map/adam_chunk/pallas_call | solution.py:224
  37.2 1.2 %collective-permute-done.8.refs_0_ = bf16[256,1024]{1,0:T(8,128)(2,1)S(1)} collective-permute-done((bf16[256,1024]{1,0:T(8,128)(2,1)S(1)}, bf16[256,1024]{1,0:T(8,128)(2,1)S(1)}, u32[]{:S(2)}, u32[]{:S(2)}) %collective-permute-start.8) | collective-permute-done | bytes 524320 | tf_op jit(solution)/shard_map/ppermute | solution.py:24
  39.5 2.6 %weight_update.7 = (f32[4096,256]{1,0:T(8,128)S(1)}, f32[4096,256]{1,0:T(8,128)S(1)}, f32[4096,256]{1,0:T(8,128)S(1)}, f32[4096,256]{1,0:T(8,128)S(1)}, bf16[16,128]{1,0:T(8,128)(2,1)S(1)}) custom-call(bf16[4096,1024]{1,0:T(8,128)(2,1)S(1)} %bitcast.1, ...), custom_call_target="tpu_custom_call", output_to_operand_aliasing={{0}: (4, {}), {1}: (5, {}), {2}: (6, {}), {3}: (7, {})} | custom-call | flops 1 | bytes 1 | tf_op jit(solution)/shard_map/weight_update/pallas_call | solution.py:324
  42.1 2.6 %adam_chunk.3 = (f32[256,2048]{1,0:T(8,128)}, f32[256,2048]{1,0:T(8,128)}, bf16[16,128]{1,0:T(8,128)(2,1)S(1)}, bf16[256,1024]{1,0:T(8,128)(2,1)S(1)}, bf16[256,...) custom-call(bf16[1024,128]{1,0:T(8,128)(2,1)S(1)} %get-tuple-element, ...), custom_call_target="tpu_custom_call", output_to_operand_aliasing={{0}: (12, {}), {1}: (13, {})} | custom-call | flops 1 | bytes 1 | tf_op jit(solution)/shard_map/adam_chunk/pallas_call | solution.py:224
  44.9 0.8 %collective-permute-start.18 = (bf16[256,1024]{1,0:T(8,128)(2,1)S(1)}, bf16[256,1024]{1,0:T(8,128)(2,1)S(1)}, u32[]{:S(2)}, u32[]{:S(2)}) collective-permute-start(bf16[256,1024]{1,0:T(8,128)(2,1)S(1)} %get-tuple-element.114.refs_0_), channel_id=1, source_target_pairs={{0,16},{8,24},{16,0},{24,8},{1,17},{9,25},{17,1},{25,9},{2,18},{10... | collective-permute-start | bytes 1572872 | tf_op jit(solution)/shard_map/ppermute | solution.py:24
  46.4 2.6 %weight_update.8 = (f32[4096,256]{1,0:T(8,128)S(1)}, f32[4096,256]{1,0:T(8,128)S(1)}, f32[4096,256]{1,0:T(8,128)S(1)}, f32[4096,256]{1,0:T(8,128)S(1)}, bf16[16,128]{1,0:T(8,128)(2,1)S(1)}) custom-call(bf16[4096,1024]{1,0:T(8,128)(2,1)S(1)} %bitcast.1, ...), custom_call_target="tpu_custom_call", output_to_operand_aliasing={{0}: (4, {}), {1}: (5, {}), {2}: (6, {}), {3}: (7, {})} | custom-call | flops 1 | bytes 1 | tf_op jit(solution)/shard_map/weight_update/pallas_call | solution.py:324
  49.0 2.8 %weight_update.9 = (f32[4096,256]{1,0:T(8,128)S(1)}, f32[4096,256]{1,0:T(8,128)S(1)}, f32[4096,256]{1,0:T(8,128)S(1)}, f32[4096,256]{1,0:T(8,128)S(1)}, bf16[16,128]{1,0:T(8,128)(2,1)S(1)}) custom-call(bf16[4096,1024]{1,0:T(8,128)(2,1)S(1)} %bitcast.1, ...), custom_call_target="tpu_custom_call", output_to_operand_aliasing={{0}: (6, {}), {1}: (7, {}), {2}: (8, {}), {3}: (9, {})} | custom-call | flops 1 | bytes 1 | tf_op jit(solution)/shard_map/weight_update/pallas_call | solution.py:324
  52.4 2.6 %weight_update.10 = (f32[4096,256]{1,0:T(8,128)S(1)}, f32[4096,256]{1,0:T(8,128)S(1)}, f32[4096,256]{1,0:T(8,128)S(1)}, f32[4096,256]{1,0:T(8,128)S(1)}, bf16[16,128]{1,0:T(8,128)(2,1)S(1)}) custom-call(bf16[4096,1024]{1,0:T(8,128)(2,1)S(1)} %bitcast.1, ...), custom_call_target="tpu_custom_call", output_to_operand_aliasing={{0}: (6, {}), {1}: (7, {}), {2}: (8, {}), {3}: (9, {})} | custom-call | flops 1 | bytes 1 | tf_op jit(solution)/shard_map/weight_update/pallas_call | solution.py:324
  55.0 6.6 %weight_update.11 = (f32[4096,2048]{1,0:T(8,128)}, f32[4096,256]{1,0:T(8,128)S(1)}, f32[4096,256]{1,0:T(8,128)S(1)}, f32[4096,256]{1,0:T(8,128)S(1)}, f32[4096,2...) custom-call(bf16[4096,1024]{1,0:T(8,128)(2,1)S(1)} %bitcast.1, ...), custom_call_target="tpu_custom_call", output_to_operand_aliasing={{1}: (4, {}), {2}: (5, {}), {3}: (6, {}), {4}: (7, {})} | custom-call | flops 1 | bytes 1 | tf_op jit(solution)/shard_map/weight_update/pallas_call | solution.py:324
  62.6 1.6 %weight_update.12 = (f32[4096,256]{1,0:T(8,128)S(1)}, f32[4096,256]{1,0:T(8,128)S(1)}, f32[4096,256]{1,0:T(8,128)S(1)}, f32[4096,256]{1,0:T(8,128)S(1)}, bf16[16,128]{1,0:T(8,128)(2,1)S(1)}) custom-call(bf16[4096,1024]{1,0:T(8,128)(2,1)S(1)} %bitcast.1, ...), custom_call_target="tpu_custom_call", output_to_operand_aliasing={{0}: (2, {}), {1}: (3, {}), {2}: (4, {}), {3}: (5, {})} | custom-call | flops 1 | bytes 1 | tf_op jit(solution)/shard_map/weight_update/pallas_call | solution.py:324
  64.2 7.0 %weight_update.13 = (f32[4096,2048]{1,0:T(8,128)}, f32[4096,256]{1,0:T(8,128)S(1)}, f32[4096,256]{1,0:T(8,128)S(1)}, f32[4096,256]{1,0:T(8,128)S(1)}, f32[4096,256]{1,0:T(8,128)S(1)}, /*index=5*/bf16[16,128]{1,0:T(8,128)(2,1)}) custom-call(bf16[4096,1024]{1,0:T(8,128)(2,1)S(1)} %bitcast.1, ...), custom_call_target="tpu_custom_call", output_to_operand_aliasing={{1}: (4, {}), {2}: (5, {}), {3}: (6, {}), {4}: (7, {}), {0}... | custom-call | flops 1 | bytes 1 | tf_op jit(solution)/shard_map/weight_update/pallas_call | solution.py:324
  (61 shorter events, 6.2 us)
Async XLA Ops:
  5.0 28.5 %collective-permute-start.7 = (bf16[256,2048]{1,0:T(8,128)(2,1)S(1)}, bf16[256,2048]{1,0:T(8,128)(2,1)S(1)}, u32[]{:S(2)}, u32[]{:S(2)}) collective-permute-start(bf16[256,2048]{1,0:T(8,128)(2,1)S(1)} %get-tuple-element.91), channel_id=1, source_target_pairs={{0,8},{8,0},{16,24},{24,16},{1,9},{9,1},{17,25},{25,17},{2,10},{10... | collective-permute-start | bytes 3145736 | tf_op jit(solution)/shard_map/ppermute | solution.py:24
  5.6 6.3 %collective-permute-start.1 = (bf16[128,256]{1,0:T(8,128)(2,1)S(1)}, bf16[128,256]{1,0:T(8,128)(2,1)S(1)}, u32[]{:S(2)}, u32[]{:S(2)}) collective-permute-start(bf16[128,256]{1,0:T(8,128)(2,1)S(1)} %get-tuple-element.83), channel_id=1, source_target_pairs={{0,16},{8,24},{16,0},{24,8},{1,17},{9,25},{17,1},{25,9},{2,18},{10... | collective-permute-start | bytes 196616 | tf_op jit(solution)/shard_map/ppermute | solution.py:24
  8.2 4.0 %collective-permute-start.2 = (bf16[128,256]{1,0:T(8,128)(2,1)S(1)}, bf16[128,256]{1,0:T(8,128)(2,1)S(1)}, u32[]{:S(2)}, u32[]{:S(2)}) collective-permute-start(bf16[128,256]{1,0:T(8,128)(2,1)S(1)} %get-tuple-element.84), channel_id=1, source_target_pairs={{0,24},{8,16},{16,8},{24,0},{1,25},{9,17},{17,9},{25,1},{2,26},{10... | collective-permute-start | bytes 196616 | tf_op jit(solution)/shard_map/ppermute | solution.py:24
  8.2 4.0 %collective-permute-start = (bf16[128,256]{1,0:T(8,128)(2,1)S(1)}, bf16[128,256]{1,0:T(8,128)(2,1)S(1)}, u32[]{:S(2)}, u32[]{:S(2)}) collective-permute-start(bf16[128,256]{1,0:T(8,128)(2,1)S(1)} %get-tuple-element.82.mark_in), channel_id=1, source_target_pairs={{0,8},{8,0},{16,24},{24,16},{1,9},{9,1},{17,25},{25,17},{2,10},{10... | collective-permute-start | bytes 196616 | tf_op jit(solution)/shard_map/ppermute | solution.py:24
  12.2 19.3 %collective-permute-start.9 = (bf16[256,1024]{1,0:T(8,128)(2,1)S(1)}, bf16[256,1024]{1,0:T(8,128)(2,1)S(1)}, u32[]{:S(2)}, u32[]{:S(2)}) collective-permute-start(bf16[256,1024]{1,0:T(8,128)(2,1)S(1)} %get-tuple-element.92.refs_2_), channel_id=1, source_target_pairs={{0,16},{8,24},{16,0},{24,8},{1,17},{9,25},{17,1},{25,9},{2,18},{10... | collective-permute-start | bytes 1572872 | tf_op jit(solution)/shard_map/ppermute | solution.py:24
  14.1 9.3 %collective-permute-start.5 = (bf16[256,128]{1,0:T(8,128)(2,1)S(1)}, bf16[256,128]{1,0:T(8,128)(2,1)S(1)}, u32[]{:S(2)}, u32[]{:S(2)}) collective-permute-start(bf16[256,128]{1,0:T(8,128)(2,1)S(1)} %share_sum.1.mark_in.refs_0_), channel_id=1, source_target_pairs={{0,6},{1,7},{2,4},{3,5},{4,2},{5,3},{6,0},{7,1},{8,14},{9,15},{10,... | collective-permute-start | bytes 196616 | tf_op jit(solution)/shard_map/ppermute | solution.py:24
  17.7 5.7 %collective-permute-start.4 = (bf16[256,128]{1,0:T(8,128)(2,1)S(1)}, bf16[256,128]{1,0:T(8,128)(2,1)S(1)}, u32[]{:S(2)}, u32[]{:S(2)}) collective-permute-start(bf16[256,128]{1,0:T(8,128)(2,1)S(1)} %share_sum.1.mark_in.refs_0_), channel_id=1, source_target_pairs={{0,4},{1,5},{2,6},{3,7},{4,0},{5,1},{6,2},{7,3},{8,12},{9,13},{10,... | collective-permute-start | bytes 196616 | tf_op jit(solution)/shard_map/ppermute | solution.py:24
  17.7 5.7 %collective-permute-start.3 = (bf16[256,128]{1,0:T(8,128)(2,1)S(1)}, bf16[256,128]{1,0:T(8,128)(2,1)S(1)}, u32[]{:S(2)}, u32[]{:S(2)}) collective-permute-start(bf16[256,128]{1,0:T(8,128)(2,1)S(1)} %share_sum.1.mark_in.refs_0_), channel_id=1, source_target_pairs={{0,2},{1,3},{2,0},{3,1},{4,6},{5,7},{6,4},{7,5},{8,10},{9,11},{10,... | collective-permute-start | bytes 196616 | tf_op jit(solution)/shard_map/ppermute | solution.py:24
  23.4 8.1 %collective-permute-start.6 = (bf16[1024,128]{1,0:T(8,128)(2,1)S(1)}, bf16[1024,128]{1,0:T(8,128)(2,1)S(1)}, u32[]{:S(2)}, u32[]{:S(2)}) collective-permute-start(bf16[1024,128]{1,0:T(8,128)(2,1)S(1)} %get-tuple-element.87.refs_0_), channel_id=1, source_target_pairs={{0,1},{1,0},{2,3},{3,2},{4,5},{5,4},{6,7},{7,6},{8,9},{9,8},{10,11... | collective-permute-start | bytes 786440 | tf_op jit(solution)/shard_map/ppermute | solution.py:24
  25.0 13.4 %collective-permute-start.8 = (bf16[256,1024]{1,0:T(8,128)(2,1)S(1)}, bf16[256,1024]{1,0:T(8,128)(2,1)S(1)}, u32[]{:S(2)}, u32[]{:S(2)}) collective-permute-start(bf16[256,1024]{1,0:T(8,128)(2,1)S(1)} %get-tuple-element.90.refs_2_), channel_id=1, source_target_pairs={{0,16},{8,24},{16,0},{24,8},{1,17},{9,25},{17,1},{25,9},{2,18},{10... | collective-permute-start | bytes 1572872 | tf_op jit(solution)/shard_map/ppermute | solution.py:24
  36.2 2.8 %collective-permute-start.16 = (bf16[256,512]{1,0:T(8,128)(2,1)S(1)}, bf16[256,512]{1,0:T(8,128)(2,1)S(1)}, u32[]{:S(2)}, u32[]{:S(2)}) collective-permute-start(bf16[256,512]{1,0:T(8,128)(2,1)S(1)} %get-tuple-element.105), channel_id=1, source_target_pairs={{0,8},{8,0},{16,24},{24,16},{1,9},{9,1},{17,25},{25,17},{2,10},{10... | collective-permute-start | bytes 786440 | tf_op jit(solution)/shard_map/ppermute | solution.py:24
  36.4 2.7 %collective-permute-start.17 = (bf16[256,512]{1,0:T(8,128)(2,1)S(1)}, bf16[256,512]{1,0:T(8,128)(2,1)S(1)}, u32[]{:S(2)}, u32[]{:S(2)}) collective-permute-start(bf16[256,512]{1,0:T(8,128)(2,1)S(1)} %get-tuple-element.106), channel_id=1, source_target_pairs={{0,8},{8,0},{16,24},{24,16},{1,9},{9,1},{17,25},{25,17},{2,10},{10... | collective-permute-start | bytes 786440 | tf_op jit(solution)/shard_map/ppermute | solution.py:24
  36.7 15.1 %collective-permute-start.19 = (bf16[256,1024]{1,0:T(8,128)(2,1)S(1)}, bf16[256,1024]{1,0:T(8,128)(2,1)S(1)}, u32[]{:S(2)}, u32[]{:S(2)}) collective-permute-start(bf16[256,1024]{1,0:T(8,128)(2,1)S(1)} %get-tuple-element.104.refs_0_), channel_id=1, source_target_pairs={{0,16},{8,24},{16,0},{24,8},{1,17},{9,25},{17,1},{25,9},{2,18},{10... | collective-permute-start | bytes 1572872 | tf_op jit(solution)/shard_map/ppermute | solution.py:24
  38.4 3.7 %collective-permute-start.12 = (bf16[256,256]{1,0:T(8,128)(2,1)S(1)}, bf16[256,256]{1,0:T(8,128)(2,1)S(1)}, u32[]{:S(2)}, u32[]{:S(2)}) collective-permute-start(bf16[256,256]{1,0:T(8,128)(2,1)S(1)} %get-tuple-element.100), channel_id=1, source_target_pairs={{0,8},{8,0},{16,24},{24,16},{1,9},{9,1},{17,25},{25,17},{2,10},{10... | collective-permute-start | bytes 393224 | tf_op jit(solution)/shard_map/ppermute | solution.py:24
  38.5 3.6 %collective-permute-start.13 = (bf16[256,256]{1,0:T(8,128)(2,1)S(1)}, bf16[256,256]{1,0:T(8,128)(2,1)S(1)}, u32[]{:S(2)}, u32[]{:S(2)}) collective-permute-start(bf16[256,256]{1,0:T(8,128)(2,1)S(1)} %get-tuple-element.101), channel_id=1, source_target_pairs={{0,8},{8,0},{16,24},{24,16},{1,9},{9,1},{17,25},{25,17},{2,10},{10... | collective-permute-start | bytes 393224 | tf_op jit(solution)/shard_map/ppermute | solution.py:24
  39.0 3.1 %collective-permute-start.14 = (bf16[256,256]{1,0:T(8,128)(2,1)S(1)}, bf16[256,256]{1,0:T(8,128)(2,1)S(1)}, u32[]{:S(2)}, u32[]{:S(2)}) collective-permute-start(bf16[256,256]{1,0:T(8,128)(2,1)S(1)} %get-tuple-element.102), channel_id=1, source_target_pairs={{0,8},{8,0},{16,24},{24,16},{1,9},{9,1},{17,25},{25,17},{2,10},{10... | collective-permute-start | bytes 393224 | tf_op jit(solution)/shard_map/ppermute | solution.py:24
  39.1 3.0 %collective-permute-start.15 = (bf16[256,256]{1,0:T(8,128)(2,1)S(1)}, bf16[256,256]{1,0:T(8,128)(2,1)S(1)}, u32[]{:S(2)}, u32[]{:S(2)}) collective-permute-start(bf16[256,256]{1,0:T(8,128)(2,1)S(1)} %get-tuple-element.103), channel_id=1, source_target_pairs={{0,8},{8,0},{16,24},{24,16},{1,9},{9,1},{17,25},{25,17},{2,10},{10... | collective-permute-start | bytes 393224 | tf_op jit(solution)/shard_map/ppermute | solution.py:24
  44.9 17.1 %collective-permute-start.18 = (bf16[256,1024]{1,0:T(8,128)(2,1)S(1)}, bf16[256,1024]{1,0:T(8,128)(2,1)S(1)}, u32[]{:S(2)}, u32[]{:S(2)}) collective-permute-start(bf16[256,1024]{1,0:T(8,128)(2,1)S(1)} %get-tuple-element.114.refs_0_), channel_id=1, source_target_pairs={{0,16},{8,24},{16,0},{24,8},{1,17},{9,25},{17,1},{25,9},{2,18},{10... | collective-permute-start | bytes 1572872 | tf_op jit(solution)/shard_map/ppermute | solution.py:24
  45.7 3.3 %collective-permute-start.21 = (bf16[256,256]{1,0:T(8,128)(2,1)S(1)}, bf16[256,256]{1,0:T(8,128)(2,1)S(1)}, u32[]{:S(2)}, u32[]{:S(2)}) collective-permute-start(bf16[256,256]{1,0:T(8,128)(2,1)S(1)} %get-tuple-element.116), channel_id=1, source_target_pairs={{0,8},{8,0},{16,24},{24,16},{1,9},{9,1},{17,25},{25,17},{2,10},{10... | collective-permute-start | bytes 393224 | tf_op jit(solution)/shard_map/ppermute | solution.py:24
  45.9 3.1 %collective-permute-start.22 = (bf16[256,256]{1,0:T(8,128)(2,1)S(1)}, bf16[256,256]{1,0:T(8,128)(2,1)S(1)}, u32[]{:S(2)}, u32[]{:S(2)}) collective-permute-start(bf16[256,256]{1,0:T(8,128)(2,1)S(1)} %get-tuple-element.117), channel_id=1, source_target_pairs={{0,8},{8,0},{16,24},{24,16},{1,9},{9,1},{17,25},{25,17},{2,10},{10... | collective-permute-start | bytes 393224 | tf_op jit(solution)/shard_map/ppermute | solution.py:24
  46.2 2.8 %collective-permute-start.23 = (bf16[256,256]{1,0:T(8,128)(2,1)S(1)}, bf16[256,256]{1,0:T(8,128)(2,1)S(1)}, u32[]{:S(2)}, u32[]{:S(2)}) collective-permute-start(bf16[256,256]{1,0:T(8,128)(2,1)S(1)} %get-tuple-element.118), channel_id=1, source_target_pairs={{0,8},{8,0},{16,24},{24,16},{1,9},{9,1},{17,25},{25,17},{2,10},{10... | collective-permute-start | bytes 393224 | tf_op jit(solution)/shard_map/ppermute | solution.py:24
  51.9 3.2 %collective-permute-start.24 = (bf16[256,512]{1,0:T(8,128)(2,1)S(1)}, bf16[256,512]{1,0:T(8,128)(2,1)S(1)}, u32[]{:S(2)}, u32[]{:S(2)}) collective-permute-start(bf16[256,512]{1,0:T(8,128)(2,1)S(1)} %get-tuple-element.131), channel_id=1, source_target_pairs={{0,8},{8,0},{16,24},{24,16},{1,9},{9,1},{17,25},{25,17},{2,10},{10... | collective-permute-start | bytes 786440 | tf_op jit(solution)/shard_map/ppermute | solution.py:24
  52.3 2.8 %collective-permute-start.25 = (bf16[256,512]{1,0:T(8,128)(2,1)S(1)}, bf16[256,512]{1,0:T(8,128)(2,1)S(1)}, u32[]{:S(2)}, u32[]{:S(2)}) collective-permute-start(bf16[256,512]{1,0:T(8,128)(2,1)S(1)} %get-tuple-element.132), channel_id=1, source_target_pairs={{0,8},{8,0},{16,24},{24,16},{1,9},{9,1},{17,25},{25,17},{2,10},{10... | collective-permute-start | bytes 786440 | tf_op jit(solution)/shard_map/ppermute | solution.py:24
  62.0 2.2 %collective-permute-start.26 = (bf16[256,512]{1,0:T(8,128)(2,1)S(1)}, bf16[256,512]{1,0:T(8,128)(2,1)S(1)}, u32[]{:S(2)}, u32[]{:S(2)}) collective-permute-start(bf16[256,512]{1,0:T(8,128)(2,1)S(1)} %get-tuple-element.144), channel_id=1, source_target_pairs={{0,8},{8,0},{16,24},{24,16},{1,9},{9,1},{17,25},{25,17},{2,10},{10... | collective-permute-start | bytes 786440 | tf_op jit(solution)/shard_map/ppermute | solution.py:24
  (8 other events, 51.3 us)
